TPU v7x, 512 devices: a whole 4x8x8 slice. The times are simulated.
512 devices in a mesh: depth: 2 (over x_lo), row: 16 (over x_hi, z), col: 16 (over y, core).
Axes of the slice: x: 4 (x_hi: 2, x_lo: 2; x = x_hi * 2 + x_lo), y: 8, z: 8, core: 2. Of those that a mesh axis runs over, the one named last changes fastest.
Arguments:
- context: bfloat16 [4096, 12288], P(('depth', 'row'), 'col'), may hold values from -6 to 6
- d_out: bfloat16 [4096, 12288], P(('depth', 'col'), 'row'), may hold values from -6 to 6
- out_weight: bfloat16 [12288, 12288], P('col', 'row'), may hold values from -0.0546875 to 0.0546875
Outputs:
- d_context: bfloat16 [4096, 12288], P(('depth', 'row'), 'col')
- d_weight: bfloat16 [12288, 12288], P('col', 'row')
All inputs are finite; a program needn't handle non-finite values.
Results may differ from a plain program's by a relative error of at most 0.02.
Values may be sent and summed in bfloat16 or wider, within the bound.
No kernel may reach another device: no remote copies, remote signals or barrier semaphores. Data moves between devices by JAX's collectives and lax.ppermute only.
A program may use at most 64 MiB of HBM per device.

v0:
```python
import jax
import jax.numpy as jnp
from jax import lax
from jax.sharding import PartitionSpec as P


def on_device(context, d_out, out_weight):
    grad_rows = lax.all_gather(d_out, "col", axis=0, tiled=True)
    d_context = lax.psum_scatter(
        lax.dot_general(
            grad_rows, out_weight, (((1,), (1,)), ((), ())), preferred_element_type=jnp.float32
        ).astype(jnp.bfloat16),
        "row",
        scatter_dimension=0,
        tiled=True,
    )
    partial_weight = lax.dot_general(
        lax.all_gather(context, "row", axis=0, tiled=True),
        grad_rows,
        (((0,), (0,)), ((), ())),
        preferred_element_type=jnp.float32,
    )
    d_weight = lax.psum(partial_weight.astype(jnp.bfloat16), "depth")
    return (d_context, d_weight)


def solution(mesh):
    in_specs = (P(("depth", "row"), "col"), P(("depth", "col"), "row"), P("col", "row"))
    out_specs = (P(("depth", "row"), "col"), P("col", "row"))
    return jax.shard_map(
        on_device, mesh=mesh, in_specs=in_specs, out_specs=out_specs, check_vma=False
    )
```

profile of v0, /device:TPU:56, one launch (start us, length us, event | category | flops | bytes accessed | tf_op | source)
XLA Modules:
  0.0 453.9 jit_solution(1605136254001172744)
XLA Ops:
  7.2 0.0 copy-start
  7.2 0.0 all-gather.5.cloned.1.call-start
  7.2 0.7 all-gather.5.cloned.1.call-update
  7.9 0.0 all-gather.3.cloned.1.call-start
  8.0 0.7 all-gather.3.cloned.1.call-update
  8.7 0.0 all-reduce.2.cloned.1.call-start
  8.7 105.8 %all-gather.5.cloned.1.call-done = bf16[2048,768]{1,0:T(8,128)(2,1)} async-done(((bf16[128,768]{1,0:T(8,128)(2,1)}), bf16[2048,768]{1,0:T(8,128)(2,1)}) %all-gather.5.cloned.1.call-update) | async-done | bytes 3145744 | tf_op jit(solution)/shard_map/all_gather | solution.py:18
  114.5 41.0 %all-gather.3.cloned.1.call-done = bf16[2048,768]{1,0:T(8,128)(2,1)} async-done(((bf16[128,768]{1,0:T(8,128)(2,1)}), bf16[2048,768]{1,0:T(8,128)(2,1)}) %all-gather.3.cloned.1.call-update) | async-done | bytes 3145744 | tf_op jit(solution)/shard_map/all_gather | solution.py:8
  155.5 6.5 %convolution_convert_fusion.1 = bf16[768,768]{1,0:T(8,128)(2,1)} fusion(bf16[2048,768]{1,0:T(8,128)(2,1)} %all-gather.5.cloned.1.call-done, bf16[2048,768]{1,0:T(8,128)(2,1)} %all-gather.3.cloned.1.call-done), kind=kOutput, calls=%fused_computation.1 | convolution fusion | flops 2416508928 | bytes 7471104 | tf_op jit(solution)/shard_map/dot_general | solution.py:17
  162.0 0.0 all-reduce.2.cloned.1.call-update
  162.1 0.0 reduce-scatter.2.cloned.1.call-start
  162.1 0.0 copy-done
  162.1 6.2 %convolution_convert_fusion = bf16[2048,768]{1,0:T(8,128)(2,1)} fusion(bf16[2048,768]{1,0:T(8,128)(2,1)} %all-gather.3.cloned.1.call-done, bf16[768,768]{1,0:T(8,128)(2,1)S(1)} %copy-done), kind=kOutput, calls=%fused_computation | convolution fusion | flops 2417491968 | bytes 7471104 | tf_op jit(solution)/shard_map/dot_general | solution.py:10
  168.3 0.0 reduce-scatter.2.cloned.1.call-update
  168.4 53.9 %all-reduce.2.cloned.1.call-done = bf16[768,768]{1,0:T(8,128)(2,1)} async-done(((bf16[768,768]{1,0:T(8,128)(2,1)}), bf16[768,768]{1,0:T(8,128)(2,1)}) %all-reduce.2.cloned.1.call-update) | async-done | bytes 1179664 | tf_op jit(solution)/shard_map/psum | solution.py:23
  222.3 222.7 %reduce-scatter.2.cloned.1.call-done = bf16[128,768]{1,0:T(8,128)(2,1)} async-done(((bf16[2048,768]{1,0:T(8,128)(2,1)}), bf16[128,768]{1,0:T(8,128)(2,1)}) %reduce-scatter.2.cloned.1.call-update) | async-done | bytes 196624 | tf_op jit(solution)/shard_map/reduce_scatter | solution.py:9
  445.0 2.4 copy.6
Async XLA Ops:
  7.2 154.9 %copy-start = (bf16[768,768]{1,0:T(8,128)(2,1)S(1)}, bf16[768,768]{1,0:T(8,128)(2,1)}, u32[]{:S(2)}) copy-start(bf16[768,768]{1,0:T(8,128)(2,1)} %param.5) | copy-start | bytes 3538948
  7.2 107.3 %all-gather.5.cloned.1.call-start = ((), (), s32[]{:S(2)}) async-start(), calls=%async_computation.3 | async-start | bytes 3342336 | tf_op jit(solution)/shard_map/all_gather | solution.py:18
  7.9 147.6 %all-gather.3.cloned.1.call-start = ((), (), s32[]{:S(2)}) async-start(), calls=%async_computation.1 | async-start | bytes 3342336 | tf_op jit(solution)/shard_map/all_gather | solution.py:8
  8.7 213.6 %all-reduce.2.cloned.1.call-start = ((), (), s32[]{:S(2)}) async-start(), calls=%async_computation.4 | async-start | bytes 2359296 | tf_op jit(solution)/shard_map/psum | solution.py:23
  162.1 283.0 %reduce-scatter.2.cloned.1.call-start = ((), (), s32[]{:S(2)}) async-start(), calls=%async_computation.2 | async-start | bytes 3342336 | tf_op jit(solution)/shard_map/reduce_scatter | solution.py:9
Sparse Core Ops, SparseCore 0:
  11.2 103.2 all-gather.4
  116.6 38.8 all-gather.2
  162.2 60.0 all-reduce.1
  228.0 217.0 reduce-scatter.1
where the time goes:
time: 455 us; the launch traced here: 454 us
  waiting for transfers between devices  425 us (93%)
  between operations  13.8 us (3%)
  matrix products  12.7 us (3%)
    reduce_scatter x1, waiting for transfers between devices, on_device(): lax.psum_scatter(lax.dot_general(grad_rows, out_weight, (((1,), (1,)), ((...  223 us
    all_gather x1, waiting for transfers between devices, on_device(): lax.all_gather(context, 'row', axis=0, tiled=True)  106 us
    psum x1, waiting for transfers between devices, on_device(): d_weight = lax.psum(partial_weight.astype(jnp.bfloat16), 'depth')  53.9 us
    all_gather x1, waiting for transfers between devices, on_device(): grad_rows = lax.all_gather(d_out, 'col', axis=0, tiled=True)  41 us
  transfers between devices with their start and end apart: 4, of which 4 were waited for; matrix products, arithmetic and copies ran while one was open for 1% of the time, Pallas kernels for 0%

commit v1 on v0

v1 whole, which is shorter than its diff:
```python
import jax
import jax.numpy as jnp
from jax import lax
from jax.experimental import pallas as pl
from jax.experimental.pallas import tpu as pltpu
from jax.sharding import PartitionSpec as P

X_HI = 2
Z = 8
Y = 8
CORES = 2
F32 = jnp.float32
BF16 = jnp.bfloat16

X_SWAP = [(i, (i + Z) % (X_HI * Z)) for i in range(X_HI * Z)]
CORE_SWAP = [(i, i ^ 1) for i in range(Y * CORES)]


def along_z(block, step):
    pairs = [(h * Z + z, h * Z + (z + step) % Z) for h in range(X_HI) for z in range(Z)]
    return lax.ppermute(block, "row", pairs)


def x_swap(block):
    return lax.ppermute(block, "row", X_SWAP)


def ring(block, other_x=0, other_core=0):
    pairs = []
    for h in range(X_HI):
        for z in range(Z):
            for y in range(Y):
                for k in range(CORES):
                    to_row = (h ^ other_x) * Z + (z + 1 - 2 * k) % Z
                    source = (h * Z + z) * Y * CORES + y * CORES + k
                    pairs.append((source, to_row * Y * CORES + y * CORES + (k ^ other_core)))
    return lax.ppermute(block, ("row", "col"), pairs)


def weight_kernel(places, *refs):
    *pieces, grad, out, total = refs
    found = [(ref, i) for ref in pieces for i in range(ref.shape[0])]
    for n in range(0, len(found), 2):
        left = jnp.concatenate([ref[i] for ref, i in found[n : n + 2]])
        right = jnp.concatenate([grad[places[n + i]] for i in range(2)])
        term = lax.dot_general(left, right, (((0,), (0,)), ((), ())), preferred_element_type=F32)
        if n == 0:
            total[...] = term
        else:
            total[...] += term
    out[...] = total[...].astype(BF16)


def weight_sum(places, pieces, grad):
    shape = (pieces[0].shape[-1], grad.shape[-1])
    in_vmem = pl.BlockSpec(memory_space=pltpu.VMEM)
    return pl.pallas_call(
        weight_kernel,
        out_shape=jax.ShapeDtypeStruct(shape, BF16),
        in_specs=[pl.BlockSpec(memory_space=pltpu.SMEM)] + [in_vmem] * (len(pieces) + 1),
        out_specs=in_vmem,
        scratch_shapes=[pltpu.VMEM(shape, F32)],
        compiler_params=pltpu.CompilerParams(vmem_limit_bytes=40 * 2**20),
        cost_estimate=pl.CostEstimate(
            flops=2 * grad.size * shape[0], bytes_accessed=4 * grad.size, transcendentals=0
        ),
        name="weight_sum",
    )(places, *pieces, grad)


def on_device(context, d_out, out_weight):
    rows, features = d_out.shape
    row, col = lax.axis_index("row"), lax.axis_index("col")
    h, z = row // Z, row % Z
    core = col % CORES
    together = lax.optimization_barrier

    grad_rows = lax.all_gather(d_out, "col", axis=0, tiled=True)

    context = context[None]
    pair = jnp.concatenate([context, along_z(context, 4)])
    weights = (out_weight, lax.ppermute(out_weight, "col", CORE_SWAP))
    pair, weights = together((pair, weights))
    up, down, x_pair = along_z(pair, 1), along_z(pair, -1), x_swap(pair)
    up, down, x_pair = together((up, down, x_pair))
    four = jnp.concatenate([up, down])
    x_four = x_swap(four)
    two = jnp.concatenate([along_z(up[:1], 1), along_z(down[:1], -1)])
    distances = jnp.array([0, 4, 7, 3, 1, 5, 6, 2])
    places = jnp.concatenate([side * Z + (z + distances) % Z for side in (h, 1 - h)])

    grad_rows, two = together((grad_rows, two))
    x_two = x_swap(two)
    blocks = grad_rows.reshape(X_HI, Z, rows, features)

    def tokens(step, x_hi=None):
        at = (z + (1 - 2 * core) * step + Z) % Z
        start = (0 if x_hi is None else x_hi, at, 0, 0)
        return lax.dynamic_slice(blocks, start, (X_HI if x_hi is None else 1, 1, rows, features))[:, 0]

    def product(grad, weight):
        return lax.dot_general(
            grad, weight, (((grad.ndim - 1,), (1,)), ((), ())), preferred_element_type=F32
        ).astype(BF16)

    half = (jnp.arange(X_HI) == core)[:, None, None]
    first = tokens(4, core)
    sums = [ring(product(first, w)) for w in weights]
    rest = jnp.stack([tokens(step) for step in (1, 2, 3)])
    partials = [product(rest, w) for w in weights]
    own = product(tokens(0), out_weight)
    keep = lax.dynamic_index_in_dim(own, h, 0, False)
    send = lax.dynamic_index_in_dim(own, 1 - h, 0, False)
    sums, partials, keep, send, x_four = together((sums, partials, keep, send, x_four))
    sums = [
        ring((p[2].astype(F32) + jnp.where(half, s.astype(F32), 0.0)).astype(BF16))
        for p, s in zip(partials, sums)
    ]

    pieces = [pair, four, two, x_pair, x_four, x_two]
    partial_weight = weight_sum(places, pieces, grad_rows.reshape(-1, rows, features))
    other_weight = lax.ppermute(partial_weight, "depth", [(0, 1), (1, 0)])

    sums, unused = together((sums, partial_weight))
    sums = [ring((p[1].astype(F32) + s.astype(F32)).astype(BF16)) for p, s in zip(partials, sums)]
    terms = [keep, x_swap(send)]
    sums, terms = together((sums, terms))
    for other_core, (p, s) in enumerate(zip(partials, sums)):
        last = (p[0].astype(F32) + s.astype(F32)).astype(BF16)
        for other_x in range(X_HI):
            part = lax.dynamic_index_in_dim(last, h ^ other_x, 0, False)
            terms.append(ring(part, other_x, other_core))
    d_context = sum(t.astype(F32) for t in terms).astype(BF16)
    d_weight = (partial_weight.astype(F32) + other_weight.astype(F32)).astype(BF16)
    return (d_context, d_weight)


def solution(mesh):
    in_specs = (P(("depth", "row"), "col"), P(("depth", "col"), "row"), P("col", "row"))
    out_specs = (P(("depth", "row"), "col"), P("col", "row"))
    return jax.shard_map(
        on_device, mesh=mesh, in_specs=in_specs, out_specs=out_specs, check_vma=False
    )
```

time: 455 us -> 152 us (0.33)
  waiting for transfers between devices: 425 us -> 48.3 us
  starting transfers between devices: 0.16 us -> 71.6 us
  matrix products: 12.7 us -> 6.29 us
  other arithmetic: 0 us -> 6.12 us
    reduce_scatter x1 -> x0, waiting for transfers between devices: 223 us -> none  [on_device(): lax.psum_scatter(lax.dot_general(grad_rows, out_weight, (((1,), (1,)), ((...]
    all_gather x1 -> x0, waiting for transfers between devices: 106 us -> none  [on_device(): lax.all_gather(context, 'row', axis=0, tiled=True)]
    ppermute x0 -> x21, starting transfers between devices: none -> 71.6 us  [the longest x5 28.5 us: along_z(): return lax.ppermute(block, 'row', pairs)]
    psum x1 -> x0, waiting for transfers between devices: 53.9 us -> none  [on_device(): d_weight = lax.psum(partial_weight.astype(jnp.bfloat16), 'depth')]
    ppermute x0 -> x21, waiting for transfers between devices: none -> 47.5 us  [the longest x5 20.5 us: along_z(): return lax.ppermute(block, 'row', pairs)]
    all_gather x1, waiting for transfers between devices: 41 us -> 0.02 us  [on_device(): grad_rows = lax.all_gather(d_out, 'col', axis=0, tiled=True)]
    dot_general x2 -> x5, matrix products: 12.7 us -> 6.29 us  [product(): lax.dot_general(grad, weight, (((grad.ndim - 1,), (1,)), ((), ())), prefe...]
    convert_element_type x0 -> x6, other arithmetic: none -> 4.96 us  [the longest x1 1.78 us: on_device(): d_context = sum((t.astype(F32) for t in terms)).astype(BF16)]
  transfers between devices with their start and end apart: 4 -> 22, of which waited for: 4 -> 12; matrix products, arithmetic and copies ran while one was open for 1% -> 8% of each run, Pallas kernels for 0% -> 2%
where the time goes in v1:
time: 152 us; the launch traced here: 151 us
  starting transfers between devices  71.6 us (47%)
  waiting for transfers between devices  48.3 us (32%)
  between operations  14.7 us (10%)
  matrix products  6.29 us (4%)
  other arithmetic  6.12 us (4%)
  Pallas kernels  3.2 us (2%)
    ppermute x5, starting transfers between devices, along_z(): return lax.ppermute(block, 'row', pairs)  28.5 us
    ppermute x10, starting transfers between devices, ring(): return lax.ppermute(block, ('row', 'col'), pairs)  25.9 us
    ppermute x5, waiting for transfers between devices, along_z(): return lax.ppermute(block, 'row', pairs)  20.5 us
    ppermute x10, waiting for transfers between devices, ring(): return lax.ppermute(block, ('row', 'col'), pairs)  14.8 us
    ppermute x4, starting transfers between devices, x_swap(): return lax.ppermute(block, 'row', X_SWAP)  12.3 us
    ppermute x4, waiting for transfers between devices, x_swap(): return lax.ppermute(block, 'row', X_SWAP)  10.5 us
    dot_general x5, matrix products, product(): lax.dot_general(grad, weight, (((grad.ndim - 1,), (1,)), ((), ())), prefe...  6.29 us
    pallas_call x1, Pallas kernels, weight_sum(): pl.pallas_call(weight_kernel, out_shape=jax.ShapeDtypeStruct(shape, BF16)...  3.2 us
  transfers between devices with their start and end apart: 22, of which 12 were waited for; matrix products, arithmetic and copies ran while one was open for 8% of the time, Pallas kernels for 2%

profile of v1, /device:TPU:56, one launch (start us, length us, event | category | flops | bytes accessed | tf_op | source)
XLA Modules:
  0.0 151.2 jit_solution(7860714254586870599)
XLA Ops:
  7.2 0.0 copy-start.9
  7.2 0.0 all-gather.2.cloned.1.call-start
  7.2 0.7 all-gather.2.cloned.1.call-update
  7.9 1.9 %collective-permute-start.1 = (bf16[768,768]{1,0:T(8,128)(2,1)}, bf16[768,768]{1,0:T(8,128)(2,1)S(1)}, u32[]{:S(2)}, u32[]{:S(2)}) collective-permute-start(bf16[768,768]{1,0:T(8,128)(2,1)} %param.6), channel_id=1, source_target_pairs={{0,1},{1,0},{2,3},{3,2},{4,5},{5,4},{6,7},{7,6},{8,9},{9,8},{10,11... | collective-permute-start | bytes 3538952 | tf_op jit(solution)/shard_map/ppermute | solution.py:82
  9.8 10.9 %collective-permute-start = (bf16[1,128,768]{2,1,0:T(8,128)(2,1)}, bf16[1,128,768]{2,1,0:T(8,128)(2,1)S(1)}, u32[]{:S(2)}, u32[]{:S(2)}) collective-permute-start(bf16[1,128,768]{2,1,0:T(8,128)(2,1)} %bitcast.85), channel_id=1, source_target_pairs={{0,64},{16,80},{32,96},{48,112},{64,0},{80,16},{96,32},{112,48},{1... | collective-permute-start | bytes 589832 | tf_op jit(solution)/shard_map/ppermute | solution.py:21
  20.8 5.9 %collective-permute-done = bf16[1,128,768]{2,1,0:T(8,128)(2,1)S(1)} collective-permute-done((bf16[1,128,768]{2,1,0:T(8,128)(2,1)}, bf16[1,128,768]{2,1,0:T(8,128)(2,1)S(1)}, u32[]{:S(2)}, u32[]{:S(2)}) %collective-permute-start) | collective-permute-done | bytes 196640 | tf_op jit(solution)/shard_map/ppermute | solution.py:21
  26.6 1.0 pad_maximum_fusion.3.refs_0_
  27.6 0.0 collective-permute-done.1
  27.6 0.0 copy-start.6
  27.6 4.9 %collective-permute-start.4 = (bf16[2,128,768]{2,1,0:T(8,128)(2,1)S(1)}, bf16[2,128,768]{2,1,0:T(8,128)(2,1)S(1)}, u32[]{:S(2)}, u32[]{:S(2)}) collective-permute-start(bf16[2,128,768]{2,1,0:T(8,128)(2,1)S(1)} %pad_maximum_fusion.3.refs_0_), channel_id=1, source_target_pairs={{0,128},{16,144},{32,160},{48,176},{64,192},{80,208},{96,224},{112... | collective-permute-start | bytes 1179656 | tf_op jit(solution)/shard_map/ppermute | solution.py:25
  32.6 9.8 %collective-permute-start.3 = (bf16[2,128,768]{2,1,0:T(8,128)(2,1)S(1)}, bf16[2,128,768]{2,1,0:T(8,128)(2,1)S(1)}, u32[]{:S(2)}, u32[]{:S(2)}) collective-permute-start(bf16[2,128,768]{2,1,0:T(8,128)(2,1)S(1)} %pad_maximum_fusion.3.refs_0_), channel_id=1, source_target_pairs={{0,112},{16,0},{32,16},{48,32},{64,48},{80,64},{96,80},{112,96},{1... | collective-permute-start | bytes 1179656 | tf_op jit(solution)/shard_map/ppermute | solution.py:21
  42.4 1.9 %collective-permute-start.2 = (bf16[2,128,768]{2,1,0:T(8,128)(2,1)S(1)}, bf16[2,128,768]{2,1,0:T(8,128)(2,1)S(1)}, u32[]{:S(2)}, u32[]{:S(2)}) collective-permute-start(bf16[2,128,768]{2,1,0:T(8,128)(2,1)S(1)} %pad_maximum_fusion.3.refs_0_), channel_id=1, source_target_pairs={{0,16},{16,32},{32,48},{48,64},{64,80},{80,96},{96,112},{112,0},{1... | collective-permute-start | bytes 1179656 | tf_op jit(solution)/shard_map/ppermute | solution.py:21
  44.5 0.0 collective-permute-done.4.refs_3_
  44.5 5.4 %collective-permute-done.3 = bf16[2,128,768]{2,1,0:T(8,128)(2,1)S(1)} collective-permute-done((bf16[2,128,768]{2,1,0:T(8,128)(2,1)S(1)}, bf16[2,128,768]{2,1,0:T(8,128)(2,1)S(1)}, u32[]{:S(2)}, u32[]{:S(2)}) %collective-permute-start.3) | collective-permute-done | bytes 393248 | tf_op jit(solution)/shard_map/ppermute | solution.py:21
  50.0 5.3 %collective-permute-done.2 = bf16[2,128,768]{2,1,0:T(8,128)(2,1)S(1)} collective-permute-done((bf16[2,128,768]{2,1,0:T(8,128)(2,1)S(1)}, bf16[2,128,768]{2,1,0:T(8,128)(2,1)S(1)}, u32[]{:S(2)}, u32[]{:S(2)}) %collective-permute-start.2) | collective-permute-done | bytes 393248 | tf_op jit(solution)/shard_map/ppermute | solution.py:21
  55.3 3.6 %collective-permute-start.6 = (bf16[1,128,768]{2,1,0:T(8,128)(2,1)S(1)}, bf16[1,128,768]{2,1,0:T(8,128)(2,1)S(1)}, u32[]{:S(2)}, u32[]{:S(2)}) collective-permute-start(bf16[1,128,768]{2,1,0:T(8,128)(2,1)S(1)} %slice.25), channel_id=1, source_target_pairs={{0,112},{16,0},{32,16},{48,32},{64,48},{80,64},{96,80},{112,96},{1... | collective-permute-start | bytes 589832 | tf_op jit(solution)/shard_map/ppermute | solution.py:21
  59.0 2.2 %collective-permute-start.5 = (bf16[1,128,768]{2,1,0:T(8,128)(2,1)S(1)}, bf16[1,128,768]{2,1,0:T(8,128)(2,1)S(1)}, u32[]{:S(2)}, u32[]{:S(2)}) collective-permute-start(bf16[1,128,768]{2,1,0:T(8,128)(2,1)S(1)} %slice.24), channel_id=1, source_target_pairs={{0,16},{16,32},{32,48},{48,64},{64,80},{80,96},{96,112},{112,0},{1... | collective-permute-start | bytes 589832 | tf_op jit(solution)/shard_map/ppermute | solution.py:21
  61.2 0.0 copy-start.3
  61.3 2.5 %collective-permute-start.9 = (bf16[4,128,768]{2,1,0:T(8,128)(2,1)S(1)}, bf16[4,128,768]{2,1,0:T(8,128)(2,1)S(1)}, u32[]{:S(2)}, u32[]{:S(2)}) collective-permute-start(bf16[4,128,768]{2,1,0:T(8,128)(2,1)S(1)} %constant_dynamic-update-slice_fusion.refs_1_), channel_id=1, source_target_pairs={{0,128},{16,144},{32,160},{48,176},{64,192},{80,208},{96,224},{112... | collective-permute-start | bytes 2359304 | tf_op jit(solution)/shard_map/ppermute | solution.py:25
  63.8 0.0 collective-permute-done.6
  63.9 3.9 %collective-permute-done.5 = bf16[1,128,768]{2,1,0:T(8,128)(2,1)S(1)} collective-permute-done((bf16[1,128,768]{2,1,0:T(8,128)(2,1)S(1)}, bf16[1,128,768]{2,1,0:T(8,128)(2,1)S(1)}, u32[]{:S(2)}, u32[]{:S(2)}) %collective-permute-start.5) | collective-permute-done | bytes 196640 | tf_op jit(solution)/shard_map/ppermute | solution.py:21
  67.8 0.0 all-gather.2.cloned.1.call-done
  67.8 2.1 %fusion.4 = bf16[1,128,768]{2,1,0:T(8,128)(2,1)S(1)} fusion(bf16[768,768]{1,0:T(8,128)(2,1)} %copy-done.6, bf16[2,8,128,768]{3,2,1,0:T(8,128)(2,1)} %bitcast.80, s32[]{:T(128)S(6)} %select_n.82, s32[]{:T(128)S(6)} %select_n.85), kind=kOutput, calls=%fused_computation.11 | convolution fusion | flops 151093248 | bytes 1572872 | tf_op jit(solution)/shard_map/dot_general | solution.py:102
  69.9 1.5 fusion.3
  71.4 2.1 %collective-permute-start.7 = (bf16[1,128,768]{2,1,0:T(8,128)(2,1)S(1)}, bf16[1,128,768]{2,1,0:T(8,128)(2,1)S(1)}, u32[]{:S(2)}, u32[]{:S(2)}) collective-permute-start(bf16[1,128,768]{2,1,0:T(8,128)(2,1)S(1)} %fusion.3), channel_id=1, source_target_pairs={{0,16},{1,113},{2,18},{3,115},{4,20},{5,117},{6,22},{7,119},{8,24}... | collective-permute-start | bytes 589832 | tf_op jit(solution)/shard_map/ppermute | solution.py:37
  73.4 1.9 %collective-permute-start.8 = (bf16[1,128,768]{2,1,0:T(8,128)(2,1)S(1)}, bf16[1,128,768]{2,1,0:T(8,128)(2,1)S(1)}, u32[]{:S(2)}, u32[]{:S(2)}) collective-permute-start(bf16[1,128,768]{2,1,0:T(8,128)(2,1)S(1)} %fusion.4), channel_id=1, source_target_pairs={{0,16},{1,113},{2,18},{3,115},{4,20},{5,117},{6,22},{7,119},{8,24}... | collective-permute-start | bytes 589832 | tf_op jit(solution)/shard_map/ppermute | solution.py:37
  75.4 0.1 dynamic-slice_bitcast_fusion.2
  75.5 1.1 convolution_convert_fusion
  76.6 0.0 copy-start.4
  76.6 1.1 convolution_convert_fusion.1
  77.8 0.5 convolution_convert_fusion.2
  78.3 2.4 %collective-permute-start.12 = (bf16[2,128,768]{2,1,0:T(8,128)(2,1)S(1)}, bf16[2,128,768]{2,1,0:T(8,128)(2,1)S(1)}, u32[]{:S(2)}, u32[]{:S(2)}) collective-permute-start(bf16[2,128,768]{2,1,0:T(8,128)(2,1)S(1)} %pad_maximum_fusion.4.refs_2_), channel_id=1, source_target_pairs={{0,128},{16,144},{32,160},{48,176},{64,192},{80,208},{96,224},{112... | collective-permute-start | bytes 1179656 | tf_op jit(solution)/shard_map/ppermute | solution.py:25
  80.7 0.8 dynamic-slice_bitcast_fusion.7
  81.5 1.6 %collective-permute-done.9.refs_4_ = bf16[4,128,768]{2,1,0:T(8,128)(2,1)S(1)} collective-permute-done((bf16[4,128,768]{2,1,0:T(8,128)(2,1)S(1)}, bf16[4,128,768]{2,1,0:T(8,128)(2,1)S(1)}, u32[]{:S(2)}, u32[]{:S(2)}) %collective-permute-start.9) | collective-permute-done | bytes 786464 | tf_op jit(solution)/shard_map/ppermute | solution.py:25
  83.1 0.0 collective-permute-done.7
  83.1 0.0 collective-permute-done.8
  83.2 0.3 fusion.8
  83.4 1.9 %collective-permute-start.11 = (bf16[2,128,768]{2,1,0:T(8,128)(2,1)S(1)}, bf16[2,128,768]{2,1,0:T(8,128)(2,1)S(1)}, u32[]{:S(2)}, u32[]{:S(2)}) collective-permute-start(bf16[2,128,768]{2,1,0:T(8,128)(2,1)S(1)} %get-tuple-element.55), channel_id=1, source_target_pairs={{0,16},{1,113},{2,18},{3,115},{4,20},{5,117},{6,22},{7,119},{8,24}... | collective-permute-start | bytes 1179656 | tf_op jit(solution)/shard_map/ppermute | solution.py:37
  85.4 2.5 %collective-permute-start.10 = (bf16[2,128,768]{2,1,0:T(8,128)(2,1)S(1)}, bf16[2,128,768]{2,1,0:T(8,128)(2,1)S(1)}, u32[]{:S(2)}, u32[]{:S(2)}) collective-permute-start(bf16[2,128,768]{2,1,0:T(8,128)(2,1)S(1)} %get-tuple-element.56), channel_id=1, source_target_pairs={{0,16},{1,113},{2,18},{3,115},{4,20},{5,117},{6,22},{7,119},{8,24}... | collective-permute-start | bytes 1179656 | tf_op jit(solution)/shard_map/ppermute | solution.py:37
  87.9 0.1 pad_add_fusion.places
  88.0 2.7 %collective-permute-done.12.refs_5_ = bf16[2,128,768]{2,1,0:T(8,128)(2,1)S(1)} collective-permute-done((bf16[2,128,768]{2,1,0:T(8,128)(2,1)S(1)}, bf16[2,128,768]{2,1,0:T(8,128)(2,1)S(1)}, u32[]{:S(2)}, u32[]{:S(2)}) %collective-permute-start.12) | collective-permute-done | bytes 393248 | tf_op jit(solution)/shard_map/ppermute | solution.py:25
  90.7 3.2 %weight_sum.1 = bf16[768,768]{1,0:T(8,128)(2,1)S(1)} custom-call(s32[16]{0:T(128)S(1)} %pad_add_fusion.places, bf16[2,128,768]{2,1,0:T(8,128)(2,1)S(1)} %pad_maximum_fusion.3.refs_0_, bf16[4,128,768]{2,1,0:T(8,128)(2,1)S(1)} %constant_dynamic-update-slice_fusion.refs_1_, bf16[2,128,768]{2,1,0:T(8,128)(2,1)S(1)} %pad_maximum_fusion.4.refs_2_, ...), custom_call_target="tpu_custom_call" | custom-call | flops 2415919104 | bytes 6291456 | tf_op jit(solution)/shard_map/weight_sum/pallas_call | solution.py:57
  93.9 2.3 %collective-permute-done.11 = bf16[2,128,768]{2,1,0:T(8,128)(2,1)S(1)} collective-permute-done((bf16[2,128,768]{2,1,0:T(8,128)(2,1)S(1)}, bf16[2,128,768]{2,1,0:T(8,128)(2,1)S(1)}, u32[]{:S(2)}, u32[]{:S(2)}) %collective-permute-start.11) | collective-permute-done | bytes 393248 | tf_op jit(solution)/shard_map/ppermute | solution.py:37
  96.3 4.2 %collective-permute-done.10 = bf16[2,128,768]{2,1,0:T(8,128)(2,1)S(1)} collective-permute-done((bf16[2,128,768]{2,1,0:T(8,128)(2,1)S(1)}, bf16[2,128,768]{2,1,0:T(8,128)(2,1)S(1)}, u32[]{:S(2)}, u32[]{:S(2)}) %collective-permute-start.10) | collective-permute-done | bytes 393248 | tf_op jit(solution)/shard_map/ppermute | solution.py:37
  100.5 0.1 fusion.10
  100.6 0.1 fusion.7
  100.7 1.9 %collective-permute-start.14 = (bf16[2,128,768]{2,1,0:T(8,128)(2,1)S(1)}, bf16[2,128,768]{2,1,0:T(8,128)(2,1)S(1)}, u32[]{:S(2)}, u32[]{:S(2)}) collective-permute-start(bf16[2,128,768]{2,1,0:T(8,128)(2,1)S(1)} %fusion.7), channel_id=1, source_target_pairs={{0,16},{1,113},{2,18},{3,115},{4,20},{5,117},{6,22},{7,119},{8,24}... | collective-permute-start | bytes 1179656 | tf_op jit(solution)/shard_map/ppermute | solution.py:37
  102.6 1.9 %collective-permute-start.13 = (bf16[2,128,768]{2,1,0:T(8,128)(2,1)S(1)}, bf16[2,128,768]{2,1,0:T(8,128)(2,1)}, u32[]{:S(2)}, u32[]{:S(2)}) collective-permute-start(bf16[2,128,768]{2,1,0:T(8,128)(2,1)S(1)} %fusion.10), channel_id=1, source_target_pairs={{0,16},{1,113},{2,18},{3,115},{4,20},{5,117},{6,22},{7,119},{8,24}... | collective-permute-start | bytes 1179656 | tf_op jit(solution)/shard_map/ppermute | solution.py:37
  104.5 2.4 %collective-permute-start.15 = (bf16[128,768]{1,0:T(8,128)(2,1)}, bf16[128,768]{1,0:T(8,128)(2,1)}, u32[]{:S(2)}, u32[]{:S(2)}) collective-permute-start(bf16[128,768]{1,0:T(8,128)(2,1)} %get-tuple-element.39), channel_id=1, source_target_pairs={{0,128},{16,144},{32,160},{48,176},{64,192},{80,208},{96,224},{112... | collective-permute-start | bytes 589832 | tf_op jit(solution)/shard_map/ppermute | solution.py:25
  106.9 3.0 %collective-permute-start.20 = (bf16[768,768]{1,0:T(8,128)(2,1)S(1)}, bf16[768,768]{1,0:T(8,128)(2,1)S(1)}, u32[]{:S(2)}, u32[]{:S(2)}) collective-permute-start(bf16[768,768]{1,0:T(8,128)(2,1)S(1)} %weight_sum.1), channel_id=1, source_target_pairs={{0,256},{256,0},{1,257},{257,1},{2,258},{258,2},{3,259},{259,3},{4... | collective-permute-start | bytes 3538952 | tf_op jit(solution)/shard_map/ppermute | solution.py:122
  109.9 6.2 %collective-permute-done.15 = bf16[128,768]{1,0:T(8,128)(2,1)} collective-permute-done((bf16[128,768]{1,0:T(8,128)(2,1)}, bf16[128,768]{1,0:T(8,128)(2,1)}, u32[]{:S(2)}, u32[]{:S(2)}) %collective-permute-start.15) | collective-permute-done | bytes 196640 | tf_op jit(solution)/shard_map/ppermute | solution.py:25
  116.1 0.0 collective-permute-done.14
  116.1 0.0 collective-permute-done.13
  116.1 1.4 fusion.5
  117.6 2.1 %collective-permute-start.18 = (bf16[128,768]{1,0:T(8,128)(2,1)S(1)}, bf16[128,768]{1,0:T(8,128)(2,1)S(1)}, u32[]{:S(2)}, u32[]{:S(2)}) collective-permute-start(bf16[128,768]{1,0:T(8,128)(2,1)S(1)} %get-tuple-element.51), channel_id=1, source_target_pairs={{0,17},{1,112},{2,19},{3,114},{4,21},{5,116},{6,23},{7,118},{8,25}... | collective-permute-start | bytes 589832 | tf_op jit(solution)/shard_map/ppermute | solution.py:37
  119.6 3.5 %collective-permute-start.19 = (bf16[128,768]{1,0:T(8,128)(2,1)S(1)}, bf16[128,768]{1,0:T(8,128)(2,1)S(1)}, u32[]{:S(2)}, u32[]{:S(2)}) collective-permute-start(bf16[128,768]{1,0:T(8,128)(2,1)S(1)} %get-tuple-element.52), channel_id=1, source_target_pairs={{0,145},{1,240},{2,147},{3,242},{4,149},{5,244},{6,151},{7,246},{8... | collective-permute-start | bytes 589832 | tf_op jit(solution)/shard_map/ppermute | solution.py:37
  123.2 1.9 %collective-permute-start.16 = (bf16[128,768]{1,0:T(8,128)(2,1)S(1)}, bf16[128,768]{1,0:T(8,128)(2,1)S(1)}, u32[]{:S(2)}, u32[]{:S(2)}) collective-permute-start(bf16[128,768]{1,0:T(8,128)(2,1)S(1)} %get-tuple-element.49), channel_id=1, source_target_pairs={{0,16},{1,113},{2,18},{3,115},{4,20},{5,117},{6,22},{7,119},{8,24}... | collective-permute-start | bytes 589832 | tf_op jit(solution)/shard_map/ppermute | solution.py:37
  125.2 6.2 %collective-permute-start.17 = (bf16[128,768]{1,0:T(8,128)(2,1)S(1)}, bf16[128,768]{1,0:T(8,128)(2,1)S(1)}, u32[]{:S(2)}, u32[]{:S(2)}) collective-permute-start(bf16[128,768]{1,0:T(8,128)(2,1)S(1)} %get-tuple-element.50), channel_id=1, source_target_pairs={{0,144},{1,241},{2,146},{3,243},{4,148},{5,245},{6,150},{7,247},{8... | collective-permute-start | bytes 589832 | tf_op jit(solution)/shard_map/ppermute | solution.py:37
  131.3 0.0 collective-permute-done.19
  131.4 1.5 %collective-permute-done.16 = bf16[128,768]{1,0:T(8,128)(2,1)S(1)} collective-permute-done((bf16[128,768]{1,0:T(8,128)(2,1)S(1)}, bf16[128,768]{1,0:T(8,128)(2,1)S(1)}, u32[]{:S(2)}, u32[]{:S(2)}) %collective-permute-start.16) | collective-permute-done | bytes 196640 | tf_op jit(solution)/shard_map/ppermute | solution.py:37
  132.9 6.7 %collective-permute-done.17 = bf16[128,768]{1,0:T(8,128)(2,1)S(1)} collective-permute-done((bf16[128,768]{1,0:T(8,128)(2,1)S(1)}, bf16[128,768]{1,0:T(8,128)(2,1)S(1)}, u32[]{:S(2)}, u32[]{:S(2)}) %collective-permute-start.17) | collective-permute-done | bytes 196640 | tf_op jit(solution)/shard_map/ppermute | solution.py:37
  139.6 1.8 %add_convert_fusion.1 = bf16[128,768]{1,0:T(8,128)(2,1)} fusion(bf16[128,768]{1,0:T(8,128)(2,1)S(1)} %collective-permute-done.19, bf16[128,768]{1,0:T(8,128)(2,1)S(1)} %collective-permute-done.18, bf16[128,768]{1,0:T(8,128)(2,1)S(1)} %collective-permute-done.17, bf16[128,768]{1,0:T(8,128)(2,1)S(1)} %collective-permute-done.16, ...), kind=kLoop, calls=%fused_computation.27 | loop fusion | flops 1179648 | bytes 1376256 | tf_op jit(solution)/shard_map/convert_element_type | solution.py:133
  141.3 1.7 %collective-permute-done.20 = bf16[768,768]{1,0:T(8,128)(2,1)S(1)} collective-permute-done((bf16[768,768]{1,0:T(8,128)(2,1)S(1)}, bf16[768,768]{1,0:T(8,128)(2,1)S(1)}, u32[]{:S(2)}, u32[]{:S(2)}) %collective-permute-start.20) | collective-permute-done | bytes 1179680 | tf_op jit(solution)/shard_map/ppermute | solution.py:122
  143.1 1.3 add_convert_fusion
  (29 shorter events, 0.3 us)
Async XLA Ops:
  7.2 37.3 %copy-start.9 = (s32[8]{0:T(128)S(1)}, s32[8]{0:T(128)}, u32[]{:S(2)}) copy-start(s32[8]{0:T(128)} %constant.97.clone) | copy-start | bytes 100
  7.2 60.6 %all-gather.2.cloned.1.call-start = ((), (), s32[]{:S(2)}) async-start(), calls=%async_computation | async-start | bytes 3342336 | tf_op jit(solution)/shard_map/all_gather | solution.py:78
  7.9 19.7 %collective-permute-start.1 = (bf16[768,768]{1,0:T(8,128)(2,1)}, bf16[768,768]{1,0:T(8,128)(2,1)S(1)}, u32[]{:S(2)}, u32[]{:S(2)}) collective-permute-start(bf16[768,768]{1,0:T(8,128)(2,1)} %param.6), channel_id=1, source_target_pairs={{0,1},{1,0},{2,3},{3,2},{4,5},{5,4},{6,7},{7,6},{8,9},{9,8},{10,11... | collective-permute-start | bytes 3538952 | tf_op jit(solution)/shard_map/ppermute | solution.py:82
  9.8 16.8 %collective-permute-start = (bf16[1,128,768]{2,1,0:T(8,128)(2,1)}, bf16[1,128,768]{2,1,0:T(8,128)(2,1)S(1)}, u32[]{:S(2)}, u32[]{:S(2)}) collective-permute-start(bf16[1,128,768]{2,1,0:T(8,128)(2,1)} %bitcast.85), channel_id=1, source_target_pairs={{0,64},{16,80},{32,96},{48,112},{64,0},{80,16},{96,32},{112,48},{1... | collective-permute-start | bytes 589832 | tf_op jit(solution)/shard_map/ppermute | solution.py:21
  27.6 5.0 %copy-start.6 = (bf16[768,768]{1,0:T(8,128)(2,1)}, bf16[768,768]{1,0:T(8,128)(2,1)S(1)}, u32[]{:S(2)}) copy-start(bf16[768,768]{1,0:T(8,128)(2,1)S(1)} %collective-permute-done.1) | copy-start | bytes 3538948
  27.6 16.9 %collective-permute-start.4 = (bf16[2,128,768]{2,1,0:T(8,128)(2,1)S(1)}, bf16[2,128,768]{2,1,0:T(8,128)(2,1)S(1)}, u32[]{:S(2)}, u32[]{:S(2)}) collective-permute-start(bf16[2,128,768]{2,1,0:T(8,128)(2,1)S(1)} %pad_maximum_fusion.3.refs_0_), channel_id=1, source_target_pairs={{0,128},{16,144},{32,160},{48,176},{64,192},{80,208},{96,224},{112... | collective-permute-start | bytes 1179656 | tf_op jit(solution)/shard_map/ppermute | solution.py:25
  32.6 17.4 %collective-permute-start.3 = (bf16[2,128,768]{2,1,0:T(8,128)(2,1)S(1)}, bf16[2,128,768]{2,1,0:T(8,128)(2,1)S(1)}, u32[]{:S(2)}, u32[]{:S(2)}) collective-permute-start(bf16[2,128,768]{2,1,0:T(8,128)(2,1)S(1)} %pad_maximum_fusion.3.refs_0_), channel_id=1, source_target_pairs={{0,112},{16,0},{32,16},{48,32},{64,48},{80,64},{96,80},{112,96},{1... | collective-permute-start | bytes 1179656 | tf_op jit(solution)/shard_map/ppermute | solution.py:21
  42.4 12.9 %collective-permute-start.2 = (bf16[2,128,768]{2,1,0:T(8,128)(2,1)S(1)}, bf16[2,128,768]{2,1,0:T(8,128)(2,1)S(1)}, u32[]{:S(2)}, u32[]{:S(2)}) collective-permute-start(bf16[2,128,768]{2,1,0:T(8,128)(2,1)S(1)} %pad_maximum_fusion.3.refs_0_), channel_id=1, source_target_pairs={{0,16},{16,32},{32,48},{48,64},{64,80},{80,96},{96,112},{112,0},{1... | collective-permute-start | bytes 1179656 | tf_op jit(solution)/shard_map/ppermute | solution.py:21
  44.5 16.7 %copy-start.1 = (bf16[2,128,768]{2,1,0:T(8,128)(2,1)}, bf16[2,128,768]{2,1,0:T(8,128)(2,1)S(1)}, u32[]{:S(2)}) copy-start(bf16[2,128,768]{2,1,0:T(8,128)(2,1)S(1)} %collective-permute-done.4.refs_3_) | copy-start | bytes 1179652
  55.3 8.5 %collective-permute-start.6 = (bf16[1,128,768]{2,1,0:T(8,128)(2,1)S(1)}, bf16[1,128,768]{2,1,0:T(8,128)(2,1)S(1)}, u32[]{:S(2)}, u32[]{:S(2)}) collective-permute-start(bf16[1,128,768]{2,1,0:T(8,128)(2,1)S(1)} %slice.25), channel_id=1, source_target_pairs={{0,112},{16,0},{32,16},{48,32},{64,48},{80,64},{96,80},{112,96},{1... | collective-permute-start | bytes 589832 | tf_op jit(solution)/shard_map/ppermute | solution.py:21
  59.0 8.8 %collective-permute-start.5 = (bf16[1,128,768]{2,1,0:T(8,128)(2,1)S(1)}, bf16[1,128,768]{2,1,0:T(8,128)(2,1)S(1)}, u32[]{:S(2)}, u32[]{:S(2)}) collective-permute-start(bf16[1,128,768]{2,1,0:T(8,128)(2,1)S(1)} %slice.24), channel_id=1, source_target_pairs={{0,16},{16,32},{32,48},{48,64},{64,80},{80,96},{96,112},{112,0},{1... | collective-permute-start | bytes 589832 | tf_op jit(solution)/shard_map/ppermute | solution.py:21
  61.2 8.7 %copy-start.3 = (bf16[768,768]{1,0:T(8,128)(2,1)S(1)}, bf16[768,768]{1,0:T(8,128)(2,1)}, u32[]{:S(2)}) copy-start(bf16[768,768]{1,0:T(8,128)(2,1)} %param.6) | copy-start | bytes 3538948
  61.3 21.8 %collective-permute-start.9 = (bf16[4,128,768]{2,1,0:T(8,128)(2,1)S(1)}, bf16[4,128,768]{2,1,0:T(8,128)(2,1)S(1)}, u32[]{:S(2)}, u32[]{:S(2)}) collective-permute-start(bf16[4,128,768]{2,1,0:T(8,128)(2,1)S(1)} %constant_dynamic-update-slice_fusion.refs_1_), channel_id=1, source_target_pairs={{0,128},{16,144},{32,160},{48,176},{64,192},{80,208},{96,224},{112... | collective-permute-start | bytes 2359304 | tf_op jit(solution)/shard_map/ppermute | solution.py:25
  67.8 7.6 %copy-start = (bf16[2048,768]{1,0:T(8,128)(2,1)S(1)}, bf16[2048,768]{1,0:T(8,128)(2,1)}, u32[]{:S(2)}) copy-start(bf16[2048,768]{1,0:T(8,128)(2,1)} %all-gather.2.cloned.1.call-done) | copy-start | bytes 9437188
  71.4 4.1 %copy-start.7 = (bf16[768,768]{1,0:T(8,128)(2,1)S(1)}, bf16[768,768]{1,0:T(8,128)(2,1)}, u32[]{:S(2)}) copy-start(bf16[768,768]{1,0:T(8,128)(2,1)} %copy-done.6) | copy-start | bytes 3538948
  71.4 11.7 %collective-permute-start.7 = (bf16[1,128,768]{2,1,0:T(8,128)(2,1)S(1)}, bf16[1,128,768]{2,1,0:T(8,128)(2,1)S(1)}, u32[]{:S(2)}, u32[]{:S(2)}) collective-permute-start(bf16[1,128,768]{2,1,0:T(8,128)(2,1)S(1)} %fusion.3), channel_id=1, source_target_pairs={{0,16},{1,113},{2,18},{3,115},{4,20},{5,117},{6,22},{7,119},{8,24}... | collective-permute-start | bytes 589832 | tf_op jit(solution)/shard_map/ppermute | solution.py:37
  73.4 9.6 %collective-permute-start.8 = (bf16[1,128,768]{2,1,0:T(8,128)(2,1)S(1)}, bf16[1,128,768]{2,1,0:T(8,128)(2,1)S(1)}, u32[]{:S(2)}, u32[]{:S(2)}) collective-permute-start(bf16[1,128,768]{2,1,0:T(8,128)(2,1)S(1)} %fusion.4), channel_id=1, source_target_pairs={{0,16},{1,113},{2,18},{3,115},{4,20},{5,117},{6,22},{7,119},{8,24}... | collective-permute-start | bytes 589832 | tf_op jit(solution)/shard_map/ppermute | solution.py:37
  76.6 23.9 %copy-start.4 = (bf16[3,2,128,768]{3,2,1,0:T(8,128)(2,1)}, bf16[3,2,128,768]{3,2,1,0:T(8,128)(2,1)S(1)}, u32[]{:S(2)}) copy-start(bf16[3,2,128,768]{3,2,1,0:T(8,128)(2,1)S(1)} %convolution_convert_fusion) | copy-start | bytes 3538948
  77.8 22.7 %copy-start.5 = (bf16[3,2,128,768]{3,2,1,0:T(8,128)(2,1)}, bf16[3,2,128,768]{3,2,1,0:T(8,128)(2,1)S(1)}, u32[]{:S(2)}) copy-start(bf16[3,2,128,768]{3,2,1,0:T(8,128)(2,1)S(1)} %convolution_convert_fusion.1) | copy-start | bytes 3538948
  78.3 12.4 %collective-permute-start.12 = (bf16[2,128,768]{2,1,0:T(8,128)(2,1)S(1)}, bf16[2,128,768]{2,1,0:T(8,128)(2,1)S(1)}, u32[]{:S(2)}, u32[]{:S(2)}) collective-permute-start(bf16[2,128,768]{2,1,0:T(8,128)(2,1)S(1)} %pad_maximum_fusion.4.refs_2_), channel_id=1, source_target_pairs={{0,128},{16,144},{32,160},{48,176},{64,192},{80,208},{96,224},{112... | collective-permute-start | bytes 1179656 | tf_op jit(solution)/shard_map/ppermute | solution.py:25
  83.1 7.6 %copy-start.2 = (bf16[2,128,768]{2,1,0:T(8,128)(2,1)S(1)}, bf16[2,128,768]{2,1,0:T(8,128)(2,1)}, u32[]{:S(2)}) copy-start(bf16[2,128,768]{2,1,0:T(8,128)(2,1)} %copy-done.1) | copy-start | bytes 1179652
  83.4 12.8 %collective-permute-start.11 = (bf16[2,128,768]{2,1,0:T(8,128)(2,1)S(1)}, bf16[2,128,768]{2,1,0:T(8,128)(2,1)S(1)}, u32[]{:S(2)}, u32[]{:S(2)}) collective-permute-start(bf16[2,128,768]{2,1,0:T(8,128)(2,1)S(1)} %get-tuple-element.55), channel_id=1, source_target_pairs={{0,16},{1,113},{2,18},{3,115},{4,20},{5,117},{6,22},{7,119},{8,24}... | collective-permute-start | bytes 1179656 | tf_op jit(solution)/shard_map/ppermute | solution.py:37
  85.4 15.1 %collective-permute-start.10 = (bf16[2,128,768]{2,1,0:T(8,128)(2,1)S(1)}, bf16[2,128,768]{2,1,0:T(8,128)(2,1)S(1)}, u32[]{:S(2)}, u32[]{:S(2)}) collective-permute-start(bf16[2,128,768]{2,1,0:T(8,128)(2,1)S(1)} %get-tuple-element.56), channel_id=1, source_target_pairs={{0,16},{1,113},{2,18},{3,115},{4,20},{5,117},{6,22},{7,119},{8,24}... | collective-permute-start | bytes 1179656 | tf_op jit(solution)/shard_map/ppermute | solution.py:37
  100.7 15.4 %collective-permute-start.14 = (bf16[2,128,768]{2,1,0:T(8,128)(2,1)S(1)}, bf16[2,128,768]{2,1,0:T(8,128)(2,1)S(1)}, u32[]{:S(2)}, u32[]{:S(2)}) collective-permute-start(bf16[2,128,768]{2,1,0:T(8,128)(2,1)S(1)} %fusion.7), channel_id=1, source_target_pairs={{0,16},{1,113},{2,18},{3,115},{4,20},{5,117},{6,22},{7,119},{8,24}... | collective-permute-start | bytes 1179656 | tf_op jit(solution)/shard_map/ppermute | solution.py:37
  102.6 13.5 %collective-permute-start.13 = (bf16[2,128,768]{2,1,0:T(8,128)(2,1)S(1)}, bf16[2,128,768]{2,1,0:T(8,128)(2,1)}, u32[]{:S(2)}, u32[]{:S(2)}) collective-permute-start(bf16[2,128,768]{2,1,0:T(8,128)(2,1)S(1)} %fusion.10), channel_id=1, source_target_pairs={{0,16},{1,113},{2,18},{3,115},{4,20},{5,117},{6,22},{7,119},{8,24}... | collective-permute-start | bytes 1179656 | tf_op jit(solution)/shard_map/ppermute | solution.py:37
  104.5 11.6 %collective-permute-start.15 = (bf16[128,768]{1,0:T(8,128)(2,1)}, bf16[128,768]{1,0:T(8,128)(2,1)}, u32[]{:S(2)}, u32[]{:S(2)}) collective-permute-start(bf16[128,768]{1,0:T(8,128)(2,1)} %get-tuple-element.39), channel_id=1, source_target_pairs={{0,128},{16,144},{32,160},{48,176},{64,192},{80,208},{96,224},{112... | collective-permute-start | bytes 589832 | tf_op jit(solution)/shard_map/ppermute | solution.py:25
  106.9 36.2 %collective-permute-start.20 = (bf16[768,768]{1,0:T(8,128)(2,1)S(1)}, bf16[768,768]{1,0:T(8,128)(2,1)S(1)}, u32[]{:S(2)}, u32[]{:S(2)}) collective-permute-start(bf16[768,768]{1,0:T(8,128)(2,1)S(1)} %weight_sum.1), channel_id=1, source_target_pairs={{0,256},{256,0},{1,257},{257,1},{2,258},{258,2},{3,259},{259,3},{4... | collective-permute-start | bytes 3538952 | tf_op jit(solution)/shard_map/ppermute | solution.py:122
  117.5 22.0 %copy-start.8 = (bf16[128,768]{1,0:T(8,128)(2,1)S(1)}, bf16[128,768]{1,0:T(8,128)(2,1)}, u32[]{:S(2)}) copy-start(bf16[128,768]{1,0:T(8,128)(2,1)} %get-tuple-element.40) | copy-start | bytes 589828
  117.6 13.8 %collective-permute-start.18 = (bf16[128,768]{1,0:T(8,128)(2,1)S(1)}, bf16[128,768]{1,0:T(8,128)(2,1)S(1)}, u32[]{:S(2)}, u32[]{:S(2)}) collective-permute-start(bf16[128,768]{1,0:T(8,128)(2,1)S(1)} %get-tuple-element.51), channel_id=1, source_target_pairs={{0,17},{1,112},{2,19},{3,114},{4,21},{5,116},{6,23},{7,118},{8,25}... | collective-permute-start | bytes 589832 | tf_op jit(solution)/shard_map/ppermute | solution.py:37
  119.6 11.7 %collective-permute-start.19 = (bf16[128,768]{1,0:T(8,128)(2,1)S(1)}, bf16[128,768]{1,0:T(8,128)(2,1)S(1)}, u32[]{:S(2)}, u32[]{:S(2)}) collective-permute-start(bf16[128,768]{1,0:T(8,128)(2,1)S(1)} %get-tuple-element.52), channel_id=1, source_target_pairs={{0,145},{1,240},{2,147},{3,242},{4,149},{5,244},{6,151},{7,246},{8... | collective-permute-start | bytes 589832 | tf_op jit(solution)/shard_map/ppermute | solution.py:37
  123.2 9.7 %collective-permute-start.16 = (bf16[128,768]{1,0:T(8,128)(2,1)S(1)}, bf16[128,768]{1,0:T(8,128)(2,1)S(1)}, u32[]{:S(2)}, u32[]{:S(2)}) collective-permute-start(bf16[128,768]{1,0:T(8,128)(2,1)S(1)} %get-tuple-element.49), channel_id=1, source_target_pairs={{0,16},{1,113},{2,18},{3,115},{4,20},{5,117},{6,22},{7,119},{8,24}... | collective-permute-start | bytes 589832 | tf_op jit(solution)/shard_map/ppermute | solution.py:37
  125.2 14.4 %collective-permute-start.17 = (bf16[128,768]{1,0:T(8,128)(2,1)S(1)}, bf16[128,768]{1,0:T(8,128)(2,1)S(1)}, u32[]{:S(2)}, u32[]{:S(2)}) collective-permute-start(bf16[128,768]{1,0:T(8,128)(2,1)S(1)} %get-tuple-element.50), channel_id=1, source_target_pairs={{0,144},{1,241},{2,146},{3,243},{4,148},{5,245},{6,150},{7,247},{8... | collective-permute-start | bytes 589832 | tf_op jit(solution)/shard_map/ppermute | solution.py:37
Sparse Core Ops, SparseCore 0:
  10.1 46.5 all-gather.1

commit v2 on v0

v2 whole, which is shorter than its diff:
```python
import functools

import jax
import jax.numpy as jnp
from jax import lax
from jax.experimental import pallas as pl
from jax.experimental.pallas import tpu as pltpu
from jax.sharding import PartitionSpec as P

X_HI = 2
Z = 8
Y = 8
CORES = 2
PARTS = 2
F32 = jnp.float32
BF16 = jnp.bfloat16
F16 = jnp.float16
POWERS = [12 + 8 * n for n in range(15)]
TAG_ROWS = 16

Z_GROUPS = [[h * Z + z for z in range(Z)] for h in range(X_HI)]
X_SWAP = [(i, (i + Z) % (X_HI * Z)) for i in range(X_HI * Z)]
CORE_SWAP = [(i, i ^ 1) for i in range(Y * CORES)]
IN_VMEM = pl.BlockSpec(memory_space=pltpu.VMEM)
IN_SMEM = pl.BlockSpec(memory_space=pltpu.SMEM)


def scale_kernel(block, out):
    rows = block.shape[0]
    wide = block[...].astype(F32)
    largest = jnp.max(jnp.max(jnp.abs(wide), axis=0, keepdims=True), axis=1, keepdims=True)
    n, scale = jnp.zeros((1, 1), F32), jnp.full((1, 1), 2.0 ** POWERS[0], F32)
    for power in POWERS[1:]:
        small = largest < 2.0 ** (15 - power)
        n = jnp.where(small, n + 1, n)
        scale = jnp.where(small, F32(2.0**power), scale)
    out[:rows] = (wide * scale).astype(BF16)
    out[rows:] = jnp.broadcast_to(n, (TAG_ROWS, block.shape[1])).astype(BF16)


def gather_grad(d_out):
    rows, features = d_out.shape
    (sent,) = local_call(
        scale_kernel,
        [(rows + TAG_ROWS, features)],
        0,
        in_specs=[IN_VMEM],
        out_specs=[IN_VMEM],
        name="scale_block",
    )(d_out)
    return lax.all_gather(sent.astype(F16), "col", axis=0, tiled=True)


def scaled_back(found, rows):
    found = found.reshape(-1, rows + TAG_ROWS, found.shape[1])
    n = found[:, rows, 0].astype(F32)
    back = sum(jnp.where(n == i, F32(2.0**-power), F32(0)) for i, power in enumerate(POWERS))
    return (found[:, :rows].astype(F32) * back[:, None, None]).astype(BF16)


def core_swap(block):
    return lax.ppermute(block, "col", CORE_SWAP)


def x_swap(block):
    return lax.ppermute(block, "row", X_SWAP)


def ring(block, other_x=0, other_core=0, chips=1):
    pairs = []
    for h in range(X_HI):
        for z in range(Z):
            for y in range(Y):
                for k in range(CORES):
                    to_row = (h ^ other_x) * Z + (z + chips * (1 - 2 * k)) % Z
                    source = (h * Z + z) * Y * CORES + y * CORES + k
                    pairs.append((source, to_row * Y * CORES + y * CORES + (k ^ other_core)))
    return lax.ppermute(block, ("row", "col"), pairs)


def local_call(kernel, shapes, flops, **options):
    return pl.pallas_call(
        kernel,
        out_shape=[jax.ShapeDtypeStruct(shape, BF16) for shape in shapes],
        compiler_params=pltpu.CompilerParams(vmem_limit_bytes=40 * 2**20),
        cost_estimate=pl.CostEstimate(flops=flops, bytes_accessed=2**23, transcendentals=0),
        **options,
    )


def dot(grad, weight):
    return lax.dot_general(grad, weight, (((1,), (1,)), ((), ())), preferred_element_type=F32)


def spread_kernel(block, out):
    for i in range(out.shape[0]):
        out[i] = block[...]


def first_kernel(places, here, there, far, partner, weight, other_weight, out, far_out, partner_out):
    rows, width = here.shape[1], weight.shape[0]
    grad = jnp.concatenate([here[0], there[0], far[0], partner[0]])
    found = dot(grad, weight[...]).astype(BF16)
    partner_out[...] = found[3 * rows :]
    for i in range(CORES):
        if i == 1:
            found = dot(grad[: 3 * rows], other_weight[...]).astype(BF16)
        cut = slice(i * width, (i + 1) * width)
        out[0, :, cut] = found[:rows]
        out[1, :, cut] = found[rows : 2 * rows]
        far_out[:, cut] = found[2 * rows : 3 * rows]


def pack_kernel(context, out):
    out[...] = context[:, :, : out.shape[2]]


def last_kernel(context, partner, out):
    part = out.shape[2]
    out[:Z] = context[:, :, -part:]
    for i in range(PARTS):
        out[Z + i] = partner[:, i * part : (i + 1) * part]


def near_kernel(places, grad, weight, other_weight, *outs):
    *steps, own = outs
    rows, width = grad.shape[1], weight.shape[0]
    for n, out in enumerate(steps):
        both = jnp.concatenate([grad[places[n * X_HI + i]] for i in range(X_HI)])
        for j, w in enumerate((weight, other_weight)):
            found = dot(both, w[...]).astype(BF16)
            for i in range(X_HI):
                out[i, :, j * width : (j + 1) * width] = found[i * rows : (i + 1) * rows]
    own[...] = dot(grad[places[X_HI * len(steps)]], weight[...]).astype(BF16)


def join_kernel(at, part, arrived, far, out):
    other = 1 - at[0]
    total = part[at[0]].astype(F32) + arrived[at[0]].astype(F32) + far[...].astype(F32)
    out[at[0]] = total.astype(BF16)
    out[other] = (part[other].astype(F32) + arrived[other].astype(F32)).astype(BF16)


def weight_kernel(part, x_hi, near, across, grad, out, total):
    width = out.shape[0]
    for other_x, context in enumerate((near, across)):
        cut = slice(part * width, (part + 1) * width) if other_x == 0 else slice(0, width)
        for z in range(0, Z, 2):
            left = jnp.concatenate([context[z + i, :, cut] for i in range(2)])
            at = (x_hi[0] ^ other_x) * Z + z
            right = jnp.concatenate([grad[at + i] for i in range(2)])
            term = lax.dot_general(left, right, (((0,), (0,)), ((), ())), preferred_element_type=F32)
            if other_x == 0 and z == 0:
                total[...] = term
            else:
                total[...] += term
    out[...] = total[...].astype(BF16)


def on_device(context, d_out, out_weight):
    rows, features = d_out.shape
    width = out_weight.shape[0]
    row, col = lax.axis_index("row"), lax.axis_index("col")
    h, z = row // Z, row % Z
    core = col % CORES
    together = lax.optimization_barrier

    (spread,) = local_call(
        spread_kernel,
        [(Z, rows, width)],
        0,
        in_specs=[IN_VMEM],
        out_specs=[IN_VMEM],
        name="spread_context",
    )(context)
    near = lax.all_to_all(spread, "row", 0, 0, tiled=True, axis_index_groups=Z_GROUPS)
    weights = (out_weight, core_swap(out_weight))
    found = gather_grad(d_out)
    part = width // PARTS
    (packed,) = local_call(
        pack_kernel,
        [(Z, rows, part)],
        0,
        in_specs=[IN_VMEM],
        out_specs=[IN_VMEM],
        name="pack_context",
    )(near)
    found, packed = together((found, packed))
    across = [x_swap(packed)]
    grad = scaled_back(found, rows)

    def place(step, other_x):
        return (h ^ other_x) * Z + (z + (1 - 2 * core) * step + Z) % Z

    def add(a, b):
        return (a.astype(F32) + b.astype(F32)).astype(BF16)

    block_flops = 2 * rows * features * width
    two_blocks = (X_HI, rows, CORES * width)
    far_x = h ^ core
    total, far, partner = local_call(
        first_kernel,
        [two_blocks, two_blocks[1:], (rows, width)],
        7 * block_flops,
        grid_spec=pltpu.PrefetchScalarGridSpec(
            num_scalar_prefetch=1,
            grid=(1,),
            in_specs=[
                pl.BlockSpec((1, rows, features), lambda i, places, n=n: (places[n], 0, 0))
                for n in range(4)
            ]
            + [IN_VMEM] * 2,
            out_specs=[IN_VMEM] * 3,
        ),
        name="first_products",
    )(
        jnp.stack([place(3, 0), place(3, 1), place(4, far_x), place(0, 1)]), *[grad] * 4, *weights
    )
    (packed,) = local_call(
        last_kernel,
        [(Z + PARTS, rows, part)],
        0,
        in_specs=[IN_VMEM] * 2,
        out_specs=[IN_VMEM],
        name="pack_last",
    )(near, partner)
    across.append(x_swap(packed))
    total, far = ring(total), ring(far, chips=2)
    *parts, own = local_call(
        near_kernel,
        [two_blocks] * 2 + [(rows, width)],
        9 * block_flops,
        in_specs=[IN_SMEM] + [IN_VMEM] * 3,
        out_specs=[IN_VMEM] * 3,
        name="near_products",
    )(
        jnp.stack([place(step, i) for step in (2, 1) for i in range(X_HI)] + [place(0, 0)]),
        grad,
        *weights,
    )
    terms = [own, jnp.concatenate([across[1][Z + i] for i in range(PARTS)], axis=1)]
    total, far, across[0] = together((total, far, across[0]))
    (total,) = local_call(
        join_kernel,
        [two_blocks],
        0,
        in_specs=[IN_SMEM] + [IN_VMEM] * 3,
        out_specs=[IN_VMEM],
        name="join_sums",
    )(far_x[None], parts[0], total, far)
    total = ring(total)

    weight_sums = []
    for i in range(PARTS):
        shape = (width // PARTS, features)
        weight_sums += local_call(
            functools.partial(weight_kernel, i),
            [shape],
            16 * block_flops // PARTS,
            in_specs=[IN_SMEM] + [IN_VMEM] * 3,
            out_specs=[IN_VMEM],
            scratch_shapes=[pltpu.VMEM(shape, F32)],
            name="weight_sum",
        )(h[None], near, across[i], grad)
    other_sums = [lax.ppermute(part, "depth", [(0, 1), (1, 0)]) for part in weight_sums]

    total, unused = together((total, weight_sums))
    last = add(parts[1], total)
    for other_x in range(X_HI):
        terms += [
            ring(last[other_x, :, i * width : (i + 1) * width], other_x, i) for i in range(CORES)
        ]
    terms, other_sums = together((terms, other_sums))
    d_context = sum(t.astype(F32) for t in terms).astype(BF16)
    d_weight = jnp.concatenate([add(*part) for part in zip(weight_sums, other_sums)])
    return (d_context, d_weight)


def solution(mesh):
    in_specs = (P(("depth", "row"), "col"), P(("depth", "col"), "row"), P("col", "row"))
    out_specs = (P(("depth", "row"), "col"), P("col", "row"))
    return jax.shard_map(
        on_device, mesh=mesh, in_specs=in_specs, out_specs=out_specs, check_vma=False
    )
```

time: 455 us -> 137 us (0.30)
  waiting for transfers between devices: 425 us -> 30.6 us
  starting transfers between devices: 0.16 us -> 48 us
  blocking collectives: 0 us -> 30.4 us
  Pallas kernels: 0 us -> 17.9 us
  between operations: 13.8 us -> 0.92 us
  matrix products: 12.7 us -> 0 us
  other arithmetic: 0 us -> 6.5 us
    reduce_scatter x1 -> x0, waiting for transfers between devices: 223 us -> none  [on_device(): lax.psum_scatter(lax.dot_general(grad_rows, out_weight, (((1,), (1,)), ((...]
    all_gather x2 -> x0, waiting for transfers between devices: 147 us -> none  [the longest x1 106 us: on_device(): lax.all_gather(context, 'row', axis=0, tiled=True)]
    psum x1 -> x0, waiting for transfers between devices: 53.9 us -> none  [on_device(): d_weight = lax.psum(partial_weight.astype(jnp.bfloat16), 'depth')]
    ppermute x0 -> x12, starting transfers between devices: none -> 37.5 us  [the longest x7 22.5 us: ring(): return lax.ppermute(block, ('row', 'col'), pairs)]
    all_gather x0 -> x1, blocking collectives: none -> 30.4 us  [gather_grad(): return lax.all_gather(sent.astype(F16), 'col', axis=0, tiled=True)]
    ppermute x0 -> x12, waiting for transfers between devices: none -> 23.2 us  [the longest x2 14.1 us: on_device(): lax.ppermute(part, 'depth', [(0, 1), (1, 0)])]
    pallas_call x0 -> x9, Pallas kernels: none -> 17.9 us  [the longest x2 5.18 us: on_device(): local_call(functools.partial(weight_kernel, i), [shape], 16 * block_flops...]
    dot_general x2 -> x0, matrix products: 12.7 us -> none  [the longest x1 6.52 us: on_device(): lax.dot_general(lax.all_gather(context, 'row', axis=0, tiled=True), grad_...]
  transfers between devices with their start and end apart: 4 -> 13, of which waited for: 4 -> 6; matrix products, arithmetic and copies ran while one was open for 1% -> 4% of each run, Pallas kernels for 0% -> 12%
where the time goes in v2:
time: 137 us; the launch traced here: 136 us
  starting transfers between devices  48 us (35%)
  waiting for transfers between devices  30.6 us (22%)
  blocking collectives  30.4 us (22%)
  Pallas kernels  17.9 us (13%)
  other arithmetic  6.5 us (5%)
  local copies, waits for them, and re-layouts  2.04 us (1%)
    all_gather x1, blocking collectives, gather_grad(): return lax.all_gather(sent.astype(F16), 'col', axis=0, tiled=True)  30.4 us
    ppermute x7, starting transfers between devices, ring(): return lax.ppermute(block, ('row', 'col'), pairs)  22.5 us
    ppermute x2, waiting for transfers between devices, on_device(): lax.ppermute(part, 'depth', [(0, 1), (1, 0)])  14.1 us
    all_to_all x1, starting transfers between devices, on_device(): lax.all_to_all(spread, 'row', 0, 0, tiled=True, axis_index_groups=Z_GROUPS)  10.4 us
    ppermute x7, waiting for transfers between devices, ring(): return lax.ppermute(block, ('row', 'col'), pairs)  9.05 us
    all_to_all x1, waiting for transfers between devices, on_device(): lax.all_to_all(spread, 'row', 0, 0, tiled=True, axis_index_groups=Z_GROUPS)  7.37 us
    ppermute x2, starting transfers between devices, x_swap(): return lax.ppermute(block, 'row', X_SWAP)  7.33 us
    ppermute x2, starting transfers between devices, on_device(): lax.ppermute(part, 'depth', [(0, 1), (1, 0)])  5.84 us
  transfers between devices with their start and end apart: 13, of which 6 were waited for; matrix products, arithmetic and copies ran while one was open for 4% of the time, Pallas kernels for 12%

profile of v2, /device:TPU:56, one launch (start us, length us, event | category | flops | bytes accessed | tf_op | source)
XLA Modules:
  0.0 136.2 jit_solution(16205493568017852450)
XLA Ops:
  0.6 0.0 copy-start.3
  0.6 0.9 copy-done.3
  1.6 1.3 spread_context.1
  2.8 0.0 copy-start.4
  2.8 10.4 %all-to-all-start = ((bf16[8,128,768]{2,1,0:T(8,128)(2,1)}), bf16[8,128,768]{2,1,0:T(8,128)(2,1)S(1)}, u32[]{:S(2)}, u32[]{:S(2)}) async-start(bf16[8,128,768]{2,1,0:T(8,128)(2,1)} %spread_context.1), calls=%async_computation | async-start | bytes 3145728 | tf_op jit(solution)/shard_map/all_to_all | solution.py:176
  13.3 1.9 %collective-permute-start = (bf16[768,768]{1,0:T(8,128)(2,1)}, bf16[768,768]{1,0:T(8,128)(2,1)}, u32[]{:S(2)}, u32[]{:S(2)}) collective-permute-start(bf16[768,768]{1,0:T(8,128)(2,1)} %weight.3), channel_id=1, source_target_pairs={{0,1},{1,0},{2,3},{3,2},{4,5},{5,4},{6,7},{7,6},{8,9},{9,8},{10,11... | collective-permute-start | bytes 3538952 | tf_op jit(solution)/shard_map/ppermute | solution.py:62
  15.2 0.0 copy-done.4
  15.2 0.2 scale_block.1
  15.4 30.4 %all-gather.1 = f16[2304,768]{1,0:T(8,128)(2,1)} all-gather(f16[144,768]{1,0:T(8,128)(2,1)S(1)} %convert_element_type.61), channel_id=1, replica_groups=mesh['depth'=2,'row'=16,'col'=16] {'col'}, dimensions={0}, use_global_device_ids=true | all-gather | bytes 3760128 | tf_op jit(solution)/shard_map/all_gather | solution.py:51
  45.8 0.1 pad_add_fusion.places
  45.9 7.4 %all-to-all-done.context.near = bf16[8,128,768]{2,1,0:T(8,128)(2,1)S(1)} async-done(((bf16[8,128,768]{2,1,0:T(8,128)(2,1)}), bf16[8,128,768]{2,1,0:T(8,128)(2,1)S(1)}, u32[]{:S(2)}, u32[]{:S(2)}) %all-to-all-start) | async-done | bytes 1572896 | tf_op jit(solution)/shard_map/all_to_all | solution.py:176
  53.2 0.0 copy-start
  53.2 1.0 pack_context.1
  54.2 4.9 %collective-permute-start.4 = (bf16[8,128,384]{2,1,0:T(8,128)(2,1)}, bf16[8,128,384]{2,1,0:T(8,128)(2,1)}, u32[]{:S(2)}, u32[]{:S(2)}) collective-permute-start(bf16[8,128,384]{2,1,0:T(8,128)(2,1)} %pack_context.1), channel_id=1, source_target_pairs={{0,128},{16,144},{32,160},{48,176},{64,192},{80,208},{96,224},{112... | collective-permute-start | bytes 2359304 | tf_op jit(solution)/shard_map/ppermute | solution.py:66
  59.2 0.0 copy-done
  59.2 1.0 fusion.14
  60.2 2.9 %multiply_convert_fusion.grad.here.there.far.partner = bf16[16,128,768]{2,1,0:T(8,128)(2,1)S(1)} fusion(f16[16,144,768]{2,1,0:T(8,128)(2,1)} %bitcast.25, f32[16]{0:T(128)S(1)} %fusion.14), kind=kLoop, calls=%fused_computation | loop fusion | flops 4718592 | bytes 6291520 | tf_op jit(solution)/shard_map/convert_element_type | solution.py:58
  63.1 0.0 copy-start.1
  63.1 0.0 collective-permute-done.other_weight
  63.1 4.5 %first_products.1 = (bf16[2,128,1536]{2,1,0:T(8,128)(2,1)}, bf16[128,1536]{1,0:T(8,128)(2,1)}, bf16[128,768]{1,0:T(8,128)(2,1)S(1)}) custom-call(s32[4]{0:T(128)S(1)} %pad_add_fusion.places, bf16[16,128,768]{2,1,0:T(8,128)(2,1)S(1)} %multiply_convert_fusion.grad.here.there.far.partner, ...), custom_call_target="tpu_custom_call" | custom-call | flops 1056964608 | bytes 8388608 | tf_op jit(solution)/shard_map/first_products/pallas_call | solution.py:201
  67.6 2.5 %collective-permute-start.2 = (bf16[2,128,1536]{2,1,0:T(8,128)(2,1)}, bf16[2,128,1536]{2,1,0:T(8,128)(2,1)}, u32[]{:S(2)}, u32[]{:S(2)}) collective-permute-start(bf16[2,128,1536]{2,1,0:T(8,128)(2,1)} %get-tuple-element.27), channel_id=1, source_target_pairs={{0,16},{1,113},{2,18},{3,115},{4,20},{5,117},{6,22},{7,119},{8,24}... | collective-permute-start | bytes 2359304 | tf_op jit(solution)/shard_map/ppermute | solution.py:78
  70.1 1.9 %collective-permute-start.3 = (bf16[128,1536]{1,0:T(8,128)(2,1)}, bf16[128,1536]{1,0:T(8,128)(2,1)S(1)}, u32[]{:S(2)}, u32[]{:S(2)}) collective-permute-start(bf16[128,1536]{1,0:T(8,128)(2,1)} %get-tuple-element.28), channel_id=1, source_target_pairs={{0,32},{1,97},{2,34},{3,99},{4,36},{5,101},{6,38},{7,103},{8,40},{... | collective-permute-start | bytes 1179656 | tf_op jit(solution)/shard_map/ppermute | solution.py:78
  72.0 0.0 copy-done.1
  72.0 1.0 pack_last.1
  73.0 2.4 %collective-permute-start.1 = (bf16[10,128,384]{2,1,0:T(8,128)(2,1)}, bf16[10,128,384]{2,1,0:T(8,128)(2,1)}, u32[]{:S(2)}, u32[]{:S(2)}) collective-permute-start(bf16[10,128,384]{2,1,0:T(8,128)(2,1)} %pack_last.1), channel_id=1, source_target_pairs={{0,128},{16,144},{32,160},{48,176},{64,192},{80,208},{96,224},{112... | collective-permute-start | bytes 2949128 | tf_op jit(solution)/shard_map/ppermute | solution.py:66
  75.5 0.1 stack.38.places
  75.6 3.4 %near_products.1 = (bf16[2,128,1536]{2,1,0:T(8,128)(2,1)S(1)}, bf16[2,128,1536]{2,1,0:T(8,128)(2,1)S(1)}, bf16[128,768]{1,0:T(8,128)(2,1)S(1)}) custom-call(s32[5]{0:T(128)S(1)} %stack.38.places, bf16[16,128,768]{2,1,0:T(8,128)(2,1)S(1)} %multiply_convert_fusion.grad.here.there.far.partner, bf16[768,768]{1,0:T(8,128)(2,1)} %weight.3, ...), custom_call_target="tpu_custom_call" | custom-call | flops 1358954496 | bytes 8388608 | tf_op jit(solution)/shard_map/near_products/pallas_call | solution.py:229
  79.0 0.0 copy-start.2
  79.0 7.0 %collective-permute-done.3.far = bf16[128,1536]{1,0:T(8,128)(2,1)S(1)} collective-permute-done((bf16[128,1536]{1,0:T(8,128)(2,1)}, bf16[128,1536]{1,0:T(8,128)(2,1)S(1)}, u32[]{:S(2)}, u32[]{:S(2)}) %collective-permute-start.3) | collective-permute-done | bytes 393248 | tf_op jit(solution)/shard_map/ppermute | solution.py:78
  86.0 0.0 collective-permute-done.4.across
  86.0 1.2 collective-permute-done.2.arrived
  87.2 1.4 %join_sums.1 = bf16[2,128,1536]{2,1,0:T(8,128)(2,1)S(1)} custom-call(s32[1]{0:T(128)} %bitcast.12.at, bf16[2,128,1536]{2,1,0:T(8,128)(2,1)S(1)} %get-tuple-element.26.part, bf16[2,128,1536]{2,1,0:T(8,128)(2,1)} %collective-permute-done.2.arrived, bf16[128,1536]{1,0:T(8,128)(2,1)S(1)} %collective-permute-done.3.far), custom_call_target="tpu_custom_call" | custom-call | bytes 8388608 | tf_op jit(solution)/shard_map/join_sums/pallas_call | solution.py:243
  88.6 7.5 %collective-permute-start.5 = (bf16[2,128,1536]{2,1,0:T(8,128)(2,1)S(1)}, bf16[2,128,1536]{2,1,0:T(8,128)(2,1)S(1)}, u32[]{:S(2)}, u32[]{:S(2)}) collective-permute-start(bf16[2,128,1536]{2,1,0:T(8,128)(2,1)S(1)} %join_sums.1), channel_id=1, source_target_pairs={{0,16},{1,113},{2,18},{3,115},{4,20},{5,117},{6,22},{7,119},{8,24}... | collective-permute-start | bytes 2359304 | tf_op jit(solution)/shard_map/ppermute | solution.py:78
  96.1 0.0 copy-done.2
  96.1 2.6 %weight_sum.2 = bf16[384,768]{1,0:T(8,128)(2,1)S(1)} custom-call(s32[1]{0:T(128)} %bitcast.13.x_hi, bf16[8,128,768]{2,1,0:T(8,128)(2,1)S(1)} %copy-done.2, bf16[8,128,384]{2,1,0:T(8,128)(2,1)} %collective-permute-done.4.across, bf16[16,128,768]{2,1,0:T(8,128)(2,1)S(1)} %multiply_convert_fusion.grad.here.there.far.partner), custom_call_target="tpu_custom_call" | custom-call | flops 1207959552 | bytes 8388608 | tf_op jit(solution)/shard_map/weight_sum/pallas_call | solution.py:256
  98.6 2.5 %collective-permute-start.10 = (bf16[384,768]{1,0:T(8,128)(2,1)S(1)}, bf16[384,768]{1,0:T(8,128)(2,1)S(1)}, u32[]{:S(2)}, u32[]{:S(2)}) collective-permute-start(bf16[384,768]{1,0:T(8,128)(2,1)S(1)} %weight_sum.2), channel_id=1, source_target_pairs={{0,256},{256,0},{1,257},{257,1},{2,258},{258,2},{3,259},{259,3},{4... | collective-permute-start | bytes 1769480 | tf_op jit(solution)/shard_map/ppermute | solution.py:265
  101.2 0.0 collective-permute-done.1.across
  101.2 2.6 %weight_sum.3 = bf16[384,768]{1,0:T(8,128)(2,1)S(1)} custom-call(s32[1]{0:T(128)} %bitcast.13.x_hi, bf16[8,128,768]{2,1,0:T(8,128)(2,1)S(1)} %copy-done.2, bf16[10,128,384]{2,1,0:T(8,128)(2,1)} %collective-permute-done.1.across, bf16[16,128,768]{2,1,0:T(8,128)(2,1)S(1)} %multiply_convert_fusion.grad.here.there.far.partner), custom_call_target="tpu_custom_call" | custom-call | flops 1207959552 | bytes 8388608 | tf_op jit(solution)/shard_map/weight_sum/pallas_call | solution.py:256
  103.8 3.3 %collective-permute-start.11 = (bf16[384,768]{1,0:T(8,128)(2,1)S(1)}, bf16[384,768]{1,0:T(8,128)(2,1)S(1)}, u32[]{:S(2)}, u32[]{:S(2)}) collective-permute-start(bf16[384,768]{1,0:T(8,128)(2,1)S(1)} %weight_sum.3), channel_id=1, source_target_pairs={{0,256},{256,0},{1,257},{257,1},{2,258},{258,2},{3,259},{259,3},{4... | collective-permute-start | bytes 1769480 | tf_op jit(solution)/shard_map/ppermute | solution.py:265
  107.1 0.0 collective-permute-done.5
  107.2 0.2 add_convert_fusion
  107.3 0.1 slice_bitcast_fusion
  107.4 1.9 %collective-permute-start.9 = (bf16[128,768]{1,0:T(8,128)(2,1)S(1)}, bf16[128,768]{1,0:T(8,128)(2,1)S(1)}, u32[]{:S(2)}, u32[]{:S(2)}) collective-permute-start(bf16[128,768]{1,0:T(8,128)(2,1)S(1)} %get-tuple-element.44), channel_id=1, source_target_pairs={{0,145},{1,240},{2,147},{3,242},{4,149},{5,244},{6,151},{7,246},{8... | collective-permute-start | bytes 589832 | tf_op jit(solution)/shard_map/ppermute | solution.py:78
  109.3 2.8 %collective-permute-start.8 = (bf16[128,768]{1,0:T(8,128)(2,1)S(1)}, bf16[128,768]{1,0:T(8,128)(2,1)S(1)}, u32[]{:S(2)}, u32[]{:S(2)}) collective-permute-start(bf16[128,768]{1,0:T(8,128)(2,1)S(1)} %get-tuple-element.45), channel_id=1, source_target_pairs={{0,144},{1,241},{2,146},{3,243},{4,148},{5,245},{6,150},{7,247},{8... | collective-permute-start | bytes 589832 | tf_op jit(solution)/shard_map/ppermute | solution.py:78
  112.1 4.0 %collective-permute-start.7 = (bf16[128,768]{1,0:T(8,128)(2,1)S(1)}, bf16[128,768]{1,0:T(8,128)(2,1)S(1)}, u32[]{:S(2)}, u32[]{:S(2)}) collective-permute-start(bf16[128,768]{1,0:T(8,128)(2,1)S(1)} %get-tuple-element.46), channel_id=1, source_target_pairs={{0,17},{1,112},{2,19},{3,114},{4,21},{5,116},{6,23},{7,118},{8,25}... | collective-permute-start | bytes 589832 | tf_op jit(solution)/shard_map/ppermute | solution.py:78
  116.1 9.1 %collective-permute-done.10 = bf16[384,768]{1,0:T(8,128)(2,1)S(1)} collective-permute-done((bf16[384,768]{1,0:T(8,128)(2,1)S(1)}, bf16[384,768]{1,0:T(8,128)(2,1)S(1)}, u32[]{:S(2)}, u32[]{:S(2)}) %collective-permute-start.10) | collective-permute-done | bytes 589856 | tf_op jit(solution)/shard_map/ppermute | solution.py:265
  125.2 1.9 %collective-permute-start.6 = (bf16[128,768]{1,0:T(8,128)(2,1)S(1)}, bf16[128,768]{1,0:T(8,128)(2,1)S(1)}, u32[]{:S(2)}, u32[]{:S(2)}) collective-permute-start(bf16[128,768]{1,0:T(8,128)(2,1)S(1)} %get-tuple-element.47), channel_id=1, source_target_pairs={{0,16},{1,113},{2,18},{3,115},{4,20},{5,117},{6,22},{7,119},{8,24}... | collective-permute-start | bytes 589832 | tf_op jit(solution)/shard_map/ppermute | solution.py:78
  127.1 1.0 slice_bitcast_fusion.5
  128.1 5.0 %collective-permute-done.11 = bf16[384,768]{1,0:T(8,128)(2,1)S(1)} collective-permute-done((bf16[384,768]{1,0:T(8,128)(2,1)S(1)}, bf16[384,768]{1,0:T(8,128)(2,1)S(1)}, u32[]{:S(2)}, u32[]{:S(2)}) %collective-permute-start.11) | collective-permute-done | bytes 589856 | tf_op jit(solution)/shard_map/ppermute | solution.py:265
  133.2 0.0 collective-permute-done.9
  133.2 0.0 collective-permute-done.8
  133.2 0.0 collective-permute-done.7
  133.2 0.8 collective-permute-done.6
  134.0 0.3 add_convert_fusion.1
  134.3 1.1 pad_maximum_fusion
  135.4 0.8 add_convert_fusion.3
  (2 shorter events, 0.1 us)
Async XLA Ops:
  0.6 0.9 copy-start.3
  2.8 12.4 %copy-start.4 = (bf16[128,768]{1,0:T(8,128)(2,1)S(1)}, bf16[128,768]{1,0:T(8,128)(2,1)}, u32[]{:S(2)}) copy-start(bf16[128,768]{1,0:T(8,128)(2,1)} %block.2) | copy-start | bytes 589828
  2.8 50.4 %all-to-all-start = ((bf16[8,128,768]{2,1,0:T(8,128)(2,1)}), bf16[8,128,768]{2,1,0:T(8,128)(2,1)S(1)}, u32[]{:S(2)}, u32[]{:S(2)}) async-start(bf16[8,128,768]{2,1,0:T(8,128)(2,1)} %spread_context.1), calls=%async_computation | async-start | bytes 3145728 | tf_op jit(solution)/shard_map/all_to_all | solution.py:176
  13.3 49.9 %collective-permute-start = (bf16[768,768]{1,0:T(8,128)(2,1)}, bf16[768,768]{1,0:T(8,128)(2,1)}, u32[]{:S(2)}, u32[]{:S(2)}) collective-permute-start(bf16[768,768]{1,0:T(8,128)(2,1)} %weight.3), channel_id=1, source_target_pairs={{0,1},{1,0},{2,3},{3,2},{4,5},{5,4},{6,7},{7,6},{8,9},{9,8},{10,11... | collective-permute-start | bytes 3538952 | tf_op jit(solution)/shard_map/ppermute | solution.py:62
  53.2 5.9 %copy-start = (bf16[8,128,768]{2,1,0:T(8,128)(2,1)}, bf16[8,128,768]{2,1,0:T(8,128)(2,1)S(1)}, u32[]{:S(2)}) copy-start(bf16[8,128,768]{2,1,0:T(8,128)(2,1)S(1)} %all-to-all-done.context.near) | copy-start | bytes 4718596
  54.2 31.8 %collective-permute-start.4 = (bf16[8,128,384]{2,1,0:T(8,128)(2,1)}, bf16[8,128,384]{2,1,0:T(8,128)(2,1)}, u32[]{:S(2)}, u32[]{:S(2)}) collective-permute-start(bf16[8,128,384]{2,1,0:T(8,128)(2,1)} %pack_context.1), channel_id=1, source_target_pairs={{0,128},{16,144},{32,160},{48,176},{64,192},{80,208},{96,224},{112... | collective-permute-start | bytes 2359304 | tf_op jit(solution)/shard_map/ppermute | solution.py:66
  63.1 8.9 %copy-start.1 = (bf16[8,128,768]{2,1,0:T(8,128)(2,1)S(1)}, bf16[8,128,768]{2,1,0:T(8,128)(2,1)}, u32[]{:S(2)}) copy-start(bf16[8,128,768]{2,1,0:T(8,128)(2,1)} %copy-done) | copy-start | bytes 4718596
  67.6 19.6 %collective-permute-start.2 = (bf16[2,128,1536]{2,1,0:T(8,128)(2,1)}, bf16[2,128,1536]{2,1,0:T(8,128)(2,1)}, u32[]{:S(2)}, u32[]{:S(2)}) collective-permute-start(bf16[2,128,1536]{2,1,0:T(8,128)(2,1)} %get-tuple-element.27), channel_id=1, source_target_pairs={{0,16},{1,113},{2,18},{3,115},{4,20},{5,117},{6,22},{7,119},{8,24}... | collective-permute-start | bytes 2359304 | tf_op jit(solution)/shard_map/ppermute | solution.py:78
  70.1 16.0 %collective-permute-start.3 = (bf16[128,1536]{1,0:T(8,128)(2,1)}, bf16[128,1536]{1,0:T(8,128)(2,1)S(1)}, u32[]{:S(2)}, u32[]{:S(2)}) collective-permute-start(bf16[128,1536]{1,0:T(8,128)(2,1)} %get-tuple-element.28), channel_id=1, source_target_pairs={{0,32},{1,97},{2,34},{3,99},{4,36},{5,101},{6,38},{7,103},{8,40},{... | collective-permute-start | bytes 1179656 | tf_op jit(solution)/shard_map/ppermute | solution.py:78
  73.0 28.1 %collective-permute-start.1 = (bf16[10,128,384]{2,1,0:T(8,128)(2,1)}, bf16[10,128,384]{2,1,0:T(8,128)(2,1)}, u32[]{:S(2)}, u32[]{:S(2)}) collective-permute-start(bf16[10,128,384]{2,1,0:T(8,128)(2,1)} %pack_last.1), channel_id=1, source_target_pairs={{0,128},{16,144},{32,160},{48,176},{64,192},{80,208},{96,224},{112... | collective-permute-start | bytes 2949128 | tf_op jit(solution)/shard_map/ppermute | solution.py:66
  79.0 17.1 %copy-start.2 = (bf16[8,128,768]{2,1,0:T(8,128)(2,1)S(1)}, bf16[8,128,768]{2,1,0:T(8,128)(2,1)}, u32[]{:S(2)}) copy-start(bf16[8,128,768]{2,1,0:T(8,128)(2,1)} %copy-done) | copy-start | bytes 4718596
  88.6 18.6 %collective-permute-start.5 = (bf16[2,128,1536]{2,1,0:T(8,128)(2,1)S(1)}, bf16[2,128,1536]{2,1,0:T(8,128)(2,1)S(1)}, u32[]{:S(2)}, u32[]{:S(2)}) collective-permute-start(bf16[2,128,1536]{2,1,0:T(8,128)(2,1)S(1)} %join_sums.1), channel_id=1, source_target_pairs={{0,16},{1,113},{2,18},{3,115},{4,20},{5,117},{6,22},{7,119},{8,24}... | collective-permute-start | bytes 2359304 | tf_op jit(solution)/shard_map/ppermute | solution.py:78
  98.6 26.6 %collective-permute-start.10 = (bf16[384,768]{1,0:T(8,128)(2,1)S(1)}, bf16[384,768]{1,0:T(8,128)(2,1)S(1)}, u32[]{:S(2)}, u32[]{:S(2)}) collective-permute-start(bf16[384,768]{1,0:T(8,128)(2,1)S(1)} %weight_sum.2), channel_id=1, source_target_pairs={{0,256},{256,0},{1,257},{257,1},{2,258},{258,2},{3,259},{259,3},{4... | collective-permute-start | bytes 1769480 | tf_op jit(solution)/shard_map/ppermute | solution.py:265
  103.8 29.4 %collective-permute-start.11 = (bf16[384,768]{1,0:T(8,128)(2,1)S(1)}, bf16[384,768]{1,0:T(8,128)(2,1)S(1)}, u32[]{:S(2)}, u32[]{:S(2)}) collective-permute-start(bf16[384,768]{1,0:T(8,128)(2,1)S(1)} %weight_sum.3), channel_id=1, source_target_pairs={{0,256},{256,0},{1,257},{257,1},{2,258},{258,2},{3,259},{259,3},{4... | collective-permute-start | bytes 1769480 | tf_op jit(solution)/shard_map/ppermute | solution.py:265
  107.4 25.8 %collective-permute-start.9 = (bf16[128,768]{1,0:T(8,128)(2,1)S(1)}, bf16[128,768]{1,0:T(8,128)(2,1)S(1)}, u32[]{:S(2)}, u32[]{:S(2)}) collective-permute-start(bf16[128,768]{1,0:T(8,128)(2,1)S(1)} %get-tuple-element.44), channel_id=1, source_target_pairs={{0,145},{1,240},{2,147},{3,242},{4,149},{5,244},{6,151},{7,246},{8... | collective-permute-start | bytes 589832 | tf_op jit(solution)/shard_map/ppermute | solution.py:78
  109.3 23.8 %collective-permute-start.8 = (bf16[128,768]{1,0:T(8,128)(2,1)S(1)}, bf16[128,768]{1,0:T(8,128)(2,1)S(1)}, u32[]{:S(2)}, u32[]{:S(2)}) collective-permute-start(bf16[128,768]{1,0:T(8,128)(2,1)S(1)} %get-tuple-element.45), channel_id=1, source_target_pairs={{0,144},{1,241},{2,146},{3,243},{4,148},{5,245},{6,150},{7,247},{8... | collective-permute-start | bytes 589832 | tf_op jit(solution)/shard_map/ppermute | solution.py:78
  112.1 21.1 %collective-permute-start.7 = (bf16[128,768]{1,0:T(8,128)(2,1)S(1)}, bf16[128,768]{1,0:T(8,128)(2,1)S(1)}, u32[]{:S(2)}, u32[]{:S(2)}) collective-permute-start(bf16[128,768]{1,0:T(8,128)(2,1)S(1)} %get-tuple-element.46), channel_id=1, source_target_pairs={{0,17},{1,112},{2,19},{3,114},{4,21},{5,116},{6,23},{7,118},{8,25}... | collective-permute-start | bytes 589832 | tf_op jit(solution)/shard_map/ppermute | solution.py:78
  125.2 8.8 %collective-permute-start.6 = (bf16[128,768]{1,0:T(8,128)(2,1)S(1)}, bf16[128,768]{1,0:T(8,128)(2,1)S(1)}, u32[]{:S(2)}, u32[]{:S(2)}) collective-permute-start(bf16[128,768]{1,0:T(8,128)(2,1)S(1)} %get-tuple-element.47), channel_id=1, source_target_pairs={{0,16},{1,113},{2,18},{3,115},{4,20},{5,117},{6,22},{7,119},{8,24}... | collective-permute-start | bytes 589832 | tf_op jit(solution)/shard_map/ppermute | solution.py:78

commit v3 on v2

--- a/solution.py
+++ b/solution.py
@@ -109,10 +109,6 @@
         out[0, :, cut] = found[:rows]
         out[1, :, cut] = found[rows : 2 * rows]
         far_out[:, cut] = found[2 * rows : 3 * rows]
-
-
-def pack_kernel(context, out):
-    out[...] = context[:, :, : out.shape[2]]
 
 
 def last_kernel(context, partner, out):
@@ -174,20 +170,13 @@
         name="spread_context",
     )(context)
     near = lax.all_to_all(spread, "row", 0, 0, tiled=True, axis_index_groups=Z_GROUPS)
+    found, out_weight = together((gather_grad(d_out), out_weight))
     weights = (out_weight, core_swap(out_weight))
-    found = gather_grad(d_out)
+    grad, near = together((scaled_back(found, rows), near))
     part = width // PARTS
-    (packed,) = local_call(
-        pack_kernel,
-        [(Z, rows, part)],
-        0,
-        in_specs=[IN_VMEM],
-        out_specs=[IN_VMEM],
-        name="pack_context",
-    )(near)
-    found, packed = together((found, packed))
+    packed = near[:, :, :part]
+    grad, packed = together((grad, packed))
     across = [x_swap(packed)]
-    grad = scaled_back(found, rows)
 
     def place(step, other_x):
         return (h ^ other_x) * Z + (z + (1 - 2 * core) * step + Z) % Z
@@ -224,6 +213,7 @@
         out_specs=[IN_VMEM],
         name="pack_last",
     )(near, partner)
+    far, packed = together((far, packed))
     across.append(x_swap(packed))
     total, far = ring(total), ring(far, chips=2)
     *parts, own = local_call(
@@ -239,16 +229,6 @@
         *weights,
     )
     terms = [own, jnp.concatenate([across[1][Z + i] for i in range(PARTS)], axis=1)]
-    total, far, across[0] = together((total, far, across[0]))
-    (total,) = local_call(
-        join_kernel,
-        [two_blocks],
-        0,
-        in_specs=[IN_SMEM] + [IN_VMEM] * 3,
-        out_specs=[IN_VMEM],
-        name="join_sums",
-    )(far_x[None], parts[0], total, far)
-    total = ring(total)
 
     weight_sums = []
     for i in range(PARTS):
@@ -263,8 +243,19 @@
             name="weight_sum",
         )(h[None], near, across[i], grad)
     other_sums = [lax.ppermute(part, "depth", [(0, 1), (1, 0)]) for part in weight_sums]
-
-    total, unused = together((total, weight_sums))
+    total, far, unused = together((total, far, weight_sums[0]))
+
+    (total,) = local_call(
+        join_kernel,
+        [two_blocks],
+        0,
+        in_specs=[IN_SMEM] + [IN_VMEM] * 3,
+        out_specs=[IN_VMEM],
+        name="join_sums",
+    )(far_x[None], parts[0], total, far)
+    total = ring(total)
+
+    total, unused = together((total, weight_sums[1]))
     last = add(parts[1], total)
     for other_x in range(X_HI):
         terms += [

time: 137 us -> 134 us (0.978)
  waiting for transfers between devices: 30.6 us -> 25.7 us
  blocking collectives: 30.4 us -> 26.1 us
  starting transfers between devices: 48 us -> 51.6 us
  local copies, waits for them, and re-layouts: 2.04 us -> 4.13 us
  Pallas kernels: 17.9 us -> 19.3 us
    ppermute x7, waiting for transfers between devices: 9.05 us -> 3.81 us  [ring(): return lax.ppermute(block, ('row', 'col'), pairs)]
    ppermute x2, waiting for transfers between devices: 14.1 us -> 9.39 us  [on_device(): lax.ppermute(part, 'depth', [(0, 1), (1, 0)])]
    all_gather x1, blocking collectives: 30.4 us -> 26.1 us  [gather_grad(): return lax.all_gather(sent.astype(F16), 'col', axis=0, tiled=True)]
    ppermute x2, waiting for transfers between devices: 0.01 us -> 4.26 us  [x_swap(): return lax.ppermute(block, 'row', X_SWAP)]
    ppermute x7, starting transfers between devices: 22.5 us -> 26.6 us  [ring(): return lax.ppermute(block, ('row', 'col'), pairs)]
    slice x0 -> x1, local copies, waits for them, and re-layouts: none -> 2.1 us  [on_device(): packed = near[:, :, :part]]
    pallas_call x1, Pallas kernels: 1.03 us -> 2.44 us  [on_device(): local_call(last_kernel, [(Z + PARTS, rows, part)], 0, in_specs=[IN_VMEM]...]
  transfers between devices with their start and end apart: 13 -> 13, of which waited for: 6 -> 5; matrix products, arithmetic and copies ran while one was open for 4% -> 5% of each run, Pallas kernels for 12% -> 13%
where the time goes in v3:
time: 134 us
  starting transfers between devices  51.6 us (39%)
  blocking collectives  26.1 us (19%)
  waiting for transfers between devices  25.7 us (19%)
  Pallas kernels  19.3 us (14%)
  other arithmetic  5.76 us (4%)
  local copies, waits for them, and re-layouts  4.13 us (3%)
    ppermute x7, starting transfers between devices, ring(): return lax.ppermute(block, ('row', 'col'), pairs)  26.6 us
    all_gather x1, blocking collectives, gather_grad(): return lax.all_gather(sent.astype(F16), 'col', axis=0, tiled=True)  26.1 us
    all_to_all x1, starting transfers between devices, on_device(): lax.all_to_all(spread, 'row', 0, 0, tiled=True, axis_index_groups=Z_GROUPS)  10.4 us
    ppermute x2, waiting for transfers between devices, on_device(): lax.ppermute(part, 'depth', [(0, 1), (1, 0)])  9.39 us
    all_to_all x1, waiting for transfers between devices, on_device(): lax.all_to_all(spread, 'row', 0, 0, tiled=True, axis_index_groups=Z_GROUPS)  8.21 us
    ppermute x2, starting transfers between devices, x_swap(): return lax.ppermute(block, 'row', X_SWAP)  7.33 us
    pallas_call x2, Pallas kernels, on_device(): local_call(functools.partial(weight_kernel, i), [shape], 16 * block_flops...  6.12 us
    ppermute x2, starting transfers between devices, on_device(): lax.ppermute(part, 'depth', [(0, 1), (1, 0)])  5 us
  transfers between devices with their start and end apart: 13, of which 5 were waited for; matrix products, arithmetic and copies ran while one was open for 5% of the time, Pallas kernels for 13%

profile of v3, /device:TPU:56, one launch (start us, length us, event | category | flops | bytes accessed | tf_op | source)
XLA Modules:
  0.0 133.5 jit_solution(17378637685010576623)
XLA Ops:
  0.6 0.0 copy-start
  0.6 0.9 copy-done
  1.6 1.3 spread_context.1
  2.9 0.0 copy-start.1
  2.9 10.4 %all-to-all-start = ((bf16[8,128,768]{2,1,0:T(8,128)(2,1)}), bf16[8,128,768]{2,1,0:T(8,128)(2,1)}, u32[]{:S(2)}, u32[]{:S(2)}) async-start(bf16[8,128,768]{2,1,0:T(8,128)(2,1)} %spread_context.1), calls=%async_computation | async-start | bytes 3145728 | tf_op jit(solution)/shard_map/all_to_all | solution.py:172
  13.3 0.0 copy-done.1
  13.3 0.2 scale_block.1
  13.5 26.1 %all-gather.1 = f16[2304,768]{1,0:T(8,128)(2,1)S(1)} all-gather(f16[144,768]{1,0:T(8,128)(2,1)S(1)} %convert_element_type.61), channel_id=1, replica_groups=mesh['depth'=2,'row'=16,'col'=16] {'col'}, dimensions={0}, use_global_device_ids=true | all-gather | bytes 3760128 | tf_op jit(solution)/shard_map/all_gather | solution.py:51
  39.6 0.0 copy-start.2
  39.6 2.3 %collective-permute-start = (bf16[768,768]{1,0:T(8,128)(2,1)}, bf16[768,768]{1,0:T(8,128)(2,1)}, u32[]{:S(2)}, u32[]{:S(2)}) collective-permute-start(bf16[768,768]{1,0:T(8,128)(2,1)} %weight.1), channel_id=1, source_target_pairs={{0,1},{1,0},{2,3},{3,2},{4,5},{5,4},{6,7},{7,6},{8,9},{9,8},{10,11... | collective-permute-start | bytes 3538952 | tf_op jit(solution)/shard_map/ppermute | solution.py:62
  42.0 0.0 copy-done.2
  42.0 0.2 fusion.14
  42.2 2.9 %multiply_convert_fusion.grad.here.there.far.partner = bf16[16,128,768]{2,1,0:T(8,128)(2,1)S(1)} fusion(f16[16,144,768]{2,1,0:T(8,128)(2,1)} %bitcast.25, f32[16]{0:T(128)S(1)} %fusion.14), kind=kLoop, calls=%fused_computation | loop fusion | flops 4718592 | bytes 6291520 | tf_op jit(solution)/shard_map/convert_element_type | solution.py:58
  45.2 8.2 %all-to-all-done.context.near = bf16[8,128,768]{2,1,0:T(8,128)(2,1)} async-done(((bf16[8,128,768]{2,1,0:T(8,128)(2,1)}), bf16[8,128,768]{2,1,0:T(8,128)(2,1)}, u32[]{:S(2)}, u32[]{:S(2)}) %all-to-all-start) | async-done | bytes 1572896 | tf_op jit(solution)/shard_map/all_to_all | solution.py:172
  53.4 2.1 %slice.29 = bf16[8,128,384]{2,1,0:T(8,128)(2,1)} slice(bf16[8,128,768]{2,1,0:T(8,128)(2,1)} %all-to-all-done.context.near), slice={[0:8], [0:128], [0:384]} | slice | bytes 1572864 | tf_op jit(solution)/shard_map/slice | solution.py:177
  55.5 4.9 %collective-permute-start.4 = (bf16[8,128,384]{2,1,0:T(8,128)(2,1)}, bf16[8,128,384]{2,1,0:T(8,128)(2,1)}, u32[]{:S(2)}, u32[]{:S(2)}) collective-permute-start(bf16[8,128,384]{2,1,0:T(8,128)(2,1)} %slice.29), channel_id=1, source_target_pairs={{0,128},{16,144},{32,160},{48,176},{64,192},{80,208},{96,224},{112... | collective-permute-start | bytes 2359304 | tf_op jit(solution)/shard_map/ppermute | solution.py:66
  60.4 0.1 pad_add_fusion.places
  60.5 0.0 collective-permute-done.other_weight
  60.5 4.5 %first_products.1 = (bf16[2,128,1536]{2,1,0:T(8,128)(2,1)}, bf16[128,1536]{1,0:T(8,128)(2,1)}, bf16[128,768]{1,0:T(8,128)(2,1)S(1)}) custom-call(s32[4]{0:T(128)S(1)} %pad_add_fusion.places, bf16[16,128,768]{2,1,0:T(8,128)(2,1)S(1)} %multiply_convert_fusion.grad.here.there.far.partner, ...), custom_call_target="tpu_custom_call" | custom-call | flops 1056964608 | bytes 8388608 | tf_op jit(solution)/shard_map/first_products/pallas_call | solution.py:190
  65.0 2.5 %collective-permute-start.2 = (bf16[2,128,1536]{2,1,0:T(8,128)(2,1)}, bf16[2,128,1536]{2,1,0:T(8,128)(2,1)}, u32[]{:S(2)}, u32[]{:S(2)}) collective-permute-start(bf16[2,128,1536]{2,1,0:T(8,128)(2,1)} %get-tuple-element.38), channel_id=1, source_target_pairs={{0,16},{1,113},{2,18},{3,115},{4,20},{5,117},{6,22},{7,119},{8,24}... | collective-permute-start | bytes 2359304 | tf_op jit(solution)/shard_map/ppermute | solution.py:78
  67.5 2.4 %pack_last.1 = bf16[10,128,384]{2,1,0:T(8,128)(2,1)} custom-call(bf16[8,128,768]{2,1,0:T(8,128)(2,1)} %all-to-all-done.context.near, bf16[128,768]{1,0:T(8,128)(2,1)S(1)} %get-tuple-element.34.partner), custom_call_target="tpu_custom_call" | custom-call | bytes 8388608 | tf_op jit(solution)/shard_map/pack_last/pallas_call | solution.py:208
  69.9 1.9 %collective-permute-start.3 = (bf16[128,1536]{1,0:T(8,128)(2,1)}, bf16[128,1536]{1,0:T(8,128)(2,1)S(1)}, u32[]{:S(2)}, u32[]{:S(2)}) collective-permute-start(bf16[128,1536]{1,0:T(8,128)(2,1)} %get-tuple-element.39), channel_id=1, source_target_pairs={{0,32},{1,97},{2,34},{3,99},{4,36},{5,101},{6,38},{7,103},{8,40},{... | collective-permute-start | bytes 1179656 | tf_op jit(solution)/shard_map/ppermute | solution.py:78
  71.8 2.4 %collective-permute-start.1 = (bf16[10,128,384]{2,1,0:T(8,128)(2,1)}, bf16[10,128,384]{2,1,0:T(8,128)(2,1)}, u32[]{:S(2)}, u32[]{:S(2)}) collective-permute-start(bf16[10,128,384]{2,1,0:T(8,128)(2,1)} %pack_last.1), channel_id=1, source_target_pairs={{0,128},{16,144},{32,160},{48,176},{64,192},{80,208},{96,224},{112... | collective-permute-start | bytes 2949128 | tf_op jit(solution)/shard_map/ppermute | solution.py:66
  74.3 0.1 stack.38.places
  74.4 3.4 %near_products.1 = (bf16[2,128,1536]{2,1,0:T(8,128)(2,1)S(1)}, bf16[2,128,1536]{2,1,0:T(8,128)(2,1)S(1)}, bf16[128,768]{1,0:T(8,128)(2,1)S(1)}) custom-call(s32[5]{0:T(128)S(1)} %stack.38.places, bf16[16,128,768]{2,1,0:T(8,128)(2,1)S(1)} %multiply_convert_fusion.grad.here.there.far.partner, bf16[768,768]{1,0:T(8,128)(2,1)} %weight.1, ...), custom_call_target="tpu_custom_call" | custom-call | flops 1358954496 | bytes 8388608 | tf_op jit(solution)/shard_map/near_products/pallas_call | solution.py:219
  77.8 0.0 collective-permute-done.4.across
  77.8 3.0 %weight_sum.2 = bf16[384,768]{1,0:T(8,128)(2,1)S(1)} custom-call(s32[1]{0:T(128)} %bitcast.13.x_hi, bf16[8,128,768]{2,1,0:T(8,128)(2,1)} %all-to-all-done.context.near, bf16[8,128,384]{2,1,0:T(8,128)(2,1)} %collective-permute-done.4.across, bf16[16,128,768]{2,1,0:T(8,128)(2,1)S(1)} %multiply_convert_fusion.grad.here.there.far.partner), custom_call_target="tpu_custom_call" | custom-call | flops 1207959552 | bytes 8388608 | tf_op jit(solution)/shard_map/weight_sum/pallas_call | solution.py:236
  80.8 2.7 %collective-permute-done.3.far = bf16[128,1536]{1,0:T(8,128)(2,1)S(1)} collective-permute-done((bf16[128,1536]{1,0:T(8,128)(2,1)}, bf16[128,1536]{1,0:T(8,128)(2,1)S(1)}, u32[]{:S(2)}, u32[]{:S(2)}) %collective-permute-start.3) | collective-permute-done | bytes 393248 | tf_op jit(solution)/shard_map/ppermute | solution.py:78
  83.5 1.0 collective-permute-done.2.arrived
  84.6 1.4 %join_sums.1 = bf16[2,128,1536]{2,1,0:T(8,128)(2,1)S(1)} custom-call(s32[1]{0:T(128)} %bitcast.12.at, bf16[2,128,1536]{2,1,0:T(8,128)(2,1)S(1)} %get-tuple-element.37.part, bf16[2,128,1536]{2,1,0:T(8,128)(2,1)} %collective-permute-done.2.arrived, bf16[128,1536]{1,0:T(8,128)(2,1)S(1)} %collective-permute-done.3.far), custom_call_target="tpu_custom_call" | custom-call | bytes 8388608 | tf_op jit(solution)/shard_map/join_sums/pallas_call | solution.py:248
  86.0 7.5 %collective-permute-start.5 = (bf16[2,128,1536]{2,1,0:T(8,128)(2,1)S(1)}, bf16[2,128,1536]{2,1,0:T(8,128)(2,1)S(1)}, u32[]{:S(2)}, u32[]{:S(2)}) collective-permute-start(bf16[2,128,1536]{2,1,0:T(8,128)(2,1)S(1)} %join_sums.1), channel_id=1, source_target_pairs={{0,16},{1,113},{2,18},{3,115},{4,20},{5,117},{6,22},{7,119},{8,24}... | collective-permute-start | bytes 2359304 | tf_op jit(solution)/shard_map/ppermute | solution.py:78
  93.5 2.5 %collective-permute-start.10 = (bf16[384,768]{1,0:T(8,128)(2,1)S(1)}, bf16[384,768]{1,0:T(8,128)(2,1)S(1)}, u32[]{:S(2)}, u32[]{:S(2)}) collective-permute-start(bf16[384,768]{1,0:T(8,128)(2,1)S(1)} %weight_sum.2), channel_id=1, source_target_pairs={{0,256},{256,0},{1,257},{257,1},{2,258},{258,2},{3,259},{259,3},{4... | collective-permute-start | bytes 1769480 | tf_op jit(solution)/shard_map/ppermute | solution.py:245
  96.0 4.3 %collective-permute-done.1.across = bf16[10,128,384]{2,1,0:T(8,128)(2,1)} collective-permute-done((bf16[10,128,384]{2,1,0:T(8,128)(2,1)}, bf16[10,128,384]{2,1,0:T(8,128)(2,1)}, u32[]{:S(2)}, u32[]{:S(2)}) %collective-permute-start.1) | collective-permute-done | bytes 983072 | tf_op jit(solution)/shard_map/ppermute | solution.py:66
  100.2 3.1 %weight_sum.3 = bf16[384,768]{1,0:T(8,128)(2,1)S(1)} custom-call(s32[1]{0:T(128)} %bitcast.13.x_hi, bf16[8,128,768]{2,1,0:T(8,128)(2,1)} %all-to-all-done.context.near, bf16[10,128,384]{2,1,0:T(8,128)(2,1)} %collective-permute-done.1.across, bf16[16,128,768]{2,1,0:T(8,128)(2,1)S(1)} %multiply_convert_fusion.grad.here.there.far.partner), custom_call_target="tpu_custom_call" | custom-call | flops 1207959552 | bytes 8388608 | tf_op jit(solution)/shard_map/weight_sum/pallas_call | solution.py:236
  103.3 2.5 %collective-permute-start.11 = (bf16[384,768]{1,0:T(8,128)(2,1)S(1)}, bf16[384,768]{1,0:T(8,128)(2,1)S(1)}, u32[]{:S(2)}, u32[]{:S(2)}) collective-permute-start(bf16[384,768]{1,0:T(8,128)(2,1)S(1)} %weight_sum.3), channel_id=1, source_target_pairs={{0,256},{256,0},{1,257},{257,1},{2,258},{258,2},{3,259},{259,3},{4... | collective-permute-start | bytes 1769480 | tf_op jit(solution)/shard_map/ppermute | solution.py:245
  105.8 0.0 collective-permute-done.5
  105.8 0.2 add_convert_fusion
  106.0 0.1 slice_bitcast_fusion
  106.1 3.0 %collective-permute-start.6 = (bf16[128,768]{1,0:T(8,128)(2,1)S(1)}, bf16[128,768]{1,0:T(8,128)(2,1)S(1)}, u32[]{:S(2)}, u32[]{:S(2)}) collective-permute-start(bf16[128,768]{1,0:T(8,128)(2,1)S(1)} %get-tuple-element.57), channel_id=1, source_target_pairs={{0,16},{1,113},{2,18},{3,115},{4,20},{5,117},{6,22},{7,119},{8,24}... | collective-permute-start | bytes 589832 | tf_op jit(solution)/shard_map/ppermute | solution.py:78
  109.1 1.9 %collective-permute-start.7 = (bf16[128,768]{1,0:T(8,128)(2,1)S(1)}, bf16[128,768]{1,0:T(8,128)(2,1)S(1)}, u32[]{:S(2)}, u32[]{:S(2)}) collective-permute-start(bf16[128,768]{1,0:T(8,128)(2,1)S(1)} %get-tuple-element.56), channel_id=1, source_target_pairs={{0,17},{1,112},{2,19},{3,114},{4,21},{5,116},{6,23},{7,118},{8,25}... | collective-permute-start | bytes 589832 | tf_op jit(solution)/shard_map/ppermute | solution.py:78
  111.0 4.9 %collective-permute-start.8 = (bf16[128,768]{1,0:T(8,128)(2,1)S(1)}, bf16[128,768]{1,0:T(8,128)(2,1)S(1)}, u32[]{:S(2)}, u32[]{:S(2)}) collective-permute-start(bf16[128,768]{1,0:T(8,128)(2,1)S(1)} %get-tuple-element.55), channel_id=1, source_target_pairs={{0,144},{1,241},{2,146},{3,243},{4,148},{5,245},{6,150},{7,247},{8... | collective-permute-start | bytes 589832 | tf_op jit(solution)/shard_map/ppermute | solution.py:78
  115.9 0.0 collective-permute-done.10
  115.9 5.0 %collective-permute-start.9 = (bf16[128,768]{1,0:T(8,128)(2,1)S(1)}, bf16[128,768]{1,0:T(8,128)(2,1)S(1)}, u32[]{:S(2)}, u32[]{:S(2)}) collective-permute-start(bf16[128,768]{1,0:T(8,128)(2,1)S(1)} %get-tuple-element.54), channel_id=1, source_target_pairs={{0,145},{1,240},{2,147},{3,242},{4,149},{5,244},{6,151},{7,246},{8... | collective-permute-start | bytes 589832 | tf_op jit(solution)/shard_map/ppermute | solution.py:78
  120.9 1.0 slice_bitcast_fusion.5
  121.9 9.4 %collective-permute-done.11 = bf16[384,768]{1,0:T(8,128)(2,1)S(1)} collective-permute-done((bf16[384,768]{1,0:T(8,128)(2,1)S(1)}, bf16[384,768]{1,0:T(8,128)(2,1)S(1)}, u32[]{:S(2)}, u32[]{:S(2)}) %collective-permute-start.11) | collective-permute-done | bytes 589856 | tf_op jit(solution)/shard_map/ppermute | solution.py:245
  131.2 0.0 collective-permute-done.6
  131.2 0.0 collective-permute-done.7
  131.3 0.0 collective-permute-done.8
  131.3 0.0 collective-permute-done.9
  131.3 0.3 add_convert_fusion.1
  131.6 1.1 pad_maximum_fusion
  132.7 0.8 add_convert_fusion.3
  (2 shorter events, 0.1 us)
Async XLA Ops:
  0.6 0.9 copy-start
  2.9 10.5 %copy-start.1 = (bf16[128,768]{1,0:T(8,128)(2,1)S(1)}, bf16[128,768]{1,0:T(8,128)(2,1)}, u32[]{:S(2)}) copy-start(bf16[128,768]{1,0:T(8,128)(2,1)} %block.2) | copy-start | bytes 589828
  2.9 50.5 %all-to-all-start = ((bf16[8,128,768]{2,1,0:T(8,128)(2,1)}), bf16[8,128,768]{2,1,0:T(8,128)(2,1)}, u32[]{:S(2)}, u32[]{:S(2)}) async-start(bf16[8,128,768]{2,1,0:T(8,128)(2,1)} %spread_context.1), calls=%async_computation | async-start | bytes 3145728 | tf_op jit(solution)/shard_map/all_to_all | solution.py:172
  39.6 2.4 %copy-start.2 = (f16[2304,768]{1,0:T(8,128)(2,1)}, f16[2304,768]{1,0:T(8,128)(2,1)S(1)}, u32[]{:S(2)}) copy-start(f16[2304,768]{1,0:T(8,128)(2,1)S(1)} %all-gather.1) | copy-start | bytes 10616836
  39.6 20.9 %collective-permute-start = (bf16[768,768]{1,0:T(8,128)(2,1)}, bf16[768,768]{1,0:T(8,128)(2,1)}, u32[]{:S(2)}, u32[]{:S(2)}) collective-permute-start(bf16[768,768]{1,0:T(8,128)(2,1)} %weight.1), channel_id=1, source_target_pairs={{0,1},{1,0},{2,3},{3,2},{4,5},{5,4},{6,7},{7,6},{8,9},{9,8},{10,11... | collective-permute-start | bytes 3538952 | tf_op jit(solution)/shard_map/ppermute | solution.py:62
  55.5 22.3 %collective-permute-start.4 = (bf16[8,128,384]{2,1,0:T(8,128)(2,1)}, bf16[8,128,384]{2,1,0:T(8,128)(2,1)}, u32[]{:S(2)}, u32[]{:S(2)}) collective-permute-start(bf16[8,128,384]{2,1,0:T(8,128)(2,1)} %slice.29), channel_id=1, source_target_pairs={{0,128},{16,144},{32,160},{48,176},{64,192},{80,208},{96,224},{112... | collective-permute-start | bytes 2359304 | tf_op jit(solution)/shard_map/ppermute | solution.py:66
  65.0 19.6 %collective-permute-start.2 = (bf16[2,128,1536]{2,1,0:T(8,128)(2,1)}, bf16[2,128,1536]{2,1,0:T(8,128)(2,1)}, u32[]{:S(2)}, u32[]{:S(2)}) collective-permute-start(bf16[2,128,1536]{2,1,0:T(8,128)(2,1)} %get-tuple-element.38), channel_id=1, source_target_pairs={{0,16},{1,113},{2,18},{3,115},{4,20},{5,117},{6,22},{7,119},{8,24}... | collective-permute-start | bytes 2359304 | tf_op jit(solution)/shard_map/ppermute | solution.py:78
  69.9 13.7 %collective-permute-start.3 = (bf16[128,1536]{1,0:T(8,128)(2,1)}, bf16[128,1536]{1,0:T(8,128)(2,1)S(1)}, u32[]{:S(2)}, u32[]{:S(2)}) collective-permute-start(bf16[128,1536]{1,0:T(8,128)(2,1)} %get-tuple-element.39), channel_id=1, source_target_pairs={{0,32},{1,97},{2,34},{3,99},{4,36},{5,101},{6,38},{7,103},{8,40},{... | collective-permute-start | bytes 1179656 | tf_op jit(solution)/shard_map/ppermute | solution.py:78
  71.8 28.4 %collective-permute-start.1 = (bf16[10,128,384]{2,1,0:T(8,128)(2,1)}, bf16[10,128,384]{2,1,0:T(8,128)(2,1)}, u32[]{:S(2)}, u32[]{:S(2)}) collective-permute-start(bf16[10,128,384]{2,1,0:T(8,128)(2,1)} %pack_last.1), channel_id=1, source_target_pairs={{0,128},{16,144},{32,160},{48,176},{64,192},{80,208},{96,224},{112... | collective-permute-start | bytes 2949128 | tf_op jit(solution)/shard_map/ppermute | solution.py:66
  86.0 19.9 %collective-permute-start.5 = (bf16[2,128,1536]{2,1,0:T(8,128)(2,1)S(1)}, bf16[2,128,1536]{2,1,0:T(8,128)(2,1)S(1)}, u32[]{:S(2)}, u32[]{:S(2)}) collective-permute-start(bf16[2,128,1536]{2,1,0:T(8,128)(2,1)S(1)} %join_sums.1), channel_id=1, source_target_pairs={{0,16},{1,113},{2,18},{3,115},{4,20},{5,117},{6,22},{7,119},{8,24}... | collective-permute-start | bytes 2359304 | tf_op jit(solution)/shard_map/ppermute | solution.py:78
  93.5 22.4 %collective-permute-start.10 = (bf16[384,768]{1,0:T(8,128)(2,1)S(1)}, bf16[384,768]{1,0:T(8,128)(2,1)S(1)}, u32[]{:S(2)}, u32[]{:S(2)}) collective-permute-start(bf16[384,768]{1,0:T(8,128)(2,1)S(1)} %weight_sum.2), channel_id=1, source_target_pairs={{0,256},{256,0},{1,257},{257,1},{2,258},{258,2},{3,259},{259,3},{4... | collective-permute-start | bytes 1769480 | tf_op jit(solution)/shard_map/ppermute | solution.py:245
  103.3 27.9 %collective-permute-start.11 = (bf16[384,768]{1,0:T(8,128)(2,1)S(1)}, bf16[384,768]{1,0:T(8,128)(2,1)S(1)}, u32[]{:S(2)}, u32[]{:S(2)}) collective-permute-start(bf16[384,768]{1,0:T(8,128)(2,1)S(1)} %weight_sum.3), channel_id=1, source_target_pairs={{0,256},{256,0},{1,257},{257,1},{2,258},{258,2},{3,259},{259,3},{4... | collective-permute-start | bytes 1769480 | tf_op jit(solution)/shard_map/ppermute | solution.py:245
  106.1 25.2 %collective-permute-start.6 = (bf16[128,768]{1,0:T(8,128)(2,1)S(1)}, bf16[128,768]{1,0:T(8,128)(2,1)S(1)}, u32[]{:S(2)}, u32[]{:S(2)}) collective-permute-start(bf16[128,768]{1,0:T(8,128)(2,1)S(1)} %get-tuple-element.57), channel_id=1, source_target_pairs={{0,16},{1,113},{2,18},{3,115},{4,20},{5,117},{6,22},{7,119},{8,24}... | collective-permute-start | bytes 589832 | tf_op jit(solution)/shard_map/ppermute | solution.py:78
  109.1 22.2 %collective-permute-start.7 = (bf16[128,768]{1,0:T(8,128)(2,1)S(1)}, bf16[128,768]{1,0:T(8,128)(2,1)S(1)}, u32[]{:S(2)}, u32[]{:S(2)}) collective-permute-start(bf16[128,768]{1,0:T(8,128)(2,1)S(1)} %get-tuple-element.56), channel_id=1, source_target_pairs={{0,17},{1,112},{2,19},{3,114},{4,21},{5,116},{6,23},{7,118},{8,25}... | collective-permute-start | bytes 589832 | tf_op jit(solution)/shard_map/ppermute | solution.py:78
  111.0 20.3 %collective-permute-start.8 = (bf16[128,768]{1,0:T(8,128)(2,1)S(1)}, bf16[128,768]{1,0:T(8,128)(2,1)S(1)}, u32[]{:S(2)}, u32[]{:S(2)}) collective-permute-start(bf16[128,768]{1,0:T(8,128)(2,1)S(1)} %get-tuple-element.55), channel_id=1, source_target_pairs={{0,144},{1,241},{2,146},{3,243},{4,148},{5,245},{6,150},{7,247},{8... | collective-permute-start | bytes 589832 | tf_op jit(solution)/shard_map/ppermute | solution.py:78
  115.9 15.4 %collective-permute-start.9 = (bf16[128,768]{1,0:T(8,128)(2,1)S(1)}, bf16[128,768]{1,0:T(8,128)(2,1)S(1)}, u32[]{:S(2)}, u32[]{:S(2)}) collective-permute-start(bf16[128,768]{1,0:T(8,128)(2,1)S(1)} %get-tuple-element.54), channel_id=1, source_target_pairs={{0,145},{1,240},{2,147},{3,242},{4,149},{5,244},{6,151},{7,246},{8... | collective-permute-start | bytes 589832 | tf_op jit(solution)/shard_map/ppermute | solution.py:78

commit v4 on v3

--- a/solution.py
+++ b/solution.py
@@ -261,9 +261,12 @@
         terms += [
             ring(last[other_x, :, i * width : (i + 1) * width], other_x, i) for i in range(CORES)
         ]
-    terms, other_sums = together((terms, other_sums))
+    d_weight = lax.dynamic_update_slice(
+        jnp.zeros((width, features), BF16), add(weight_sums[0], other_sums[0]), (0, 0)
+    )
+    terms, late, d_weight = together((terms, other_sums[1], d_weight))
     d_context = sum(t.astype(F32) for t in terms).astype(BF16)
-    d_weight = jnp.concatenate([add(*part) for part in zip(weight_sums, other_sums)])
+    d_weight = lax.dynamic_update_slice(d_weight, add(weight_sums[1], late), (part, 0))
     return (d_context, d_weight)
 
 

time: 134 us -> 133 us (level)
  starting transfers between devices: 51.6 us -> 48.9 us
  waiting for transfers between devices: 25.7 us -> 28.2 us
    ppermute x7, starting transfers between devices: 26.6 us -> 22.6 us  [ring(): return lax.ppermute(block, ('row', 'col'), pairs)]
    ppermute x7, waiting for transfers between devices: 3.81 us -> 5.92 us  [ring(): return lax.ppermute(block, ('row', 'col'), pairs)]
    ppermute x2, waiting for transfers between devices: 4.26 us -> 6.36 us  [x_swap(): return lax.ppermute(block, 'row', X_SWAP)]
    ppermute x2, waiting for transfers between devices: 9.39 us -> 7.73 us  [on_device(): lax.ppermute(part, 'depth', [(0, 1), (1, 0)])]
  transfers between devices with their start and end apart: 13 -> 13, of which waited for: 5 -> 5; matrix products, arithmetic and copies ran while one was open for 5% -> 5% of each run, Pallas kernels for 13% -> 14%
where the time goes in v4:
time: 133 us; the launch traced here: 132 us
  starting transfers between devices  48.9 us (37%)
  waiting for transfers between devices  28.2 us (21%)
  blocking collectives  26.1 us (20%)
  Pallas kernels  19.3 us (15%)
  other arithmetic  4.82 us (4%)
  local copies, waits for them, and re-layouts  4.25 us (3%)
    all_gather x1, blocking collectives, gather_grad(): return lax.all_gather(sent.astype(F16), 'col', axis=0, tiled=True)  26.1 us
    ppermute x7, starting transfers between devices, ring(): return lax.ppermute(block, ('row', 'col'), pairs)  22.6 us
    all_to_all x1, starting transfers between devices, on_device(): lax.all_to_all(spread, 'row', 0, 0, tiled=True, axis_index_groups=Z_GROUPS)  10.4 us
    all_to_all x1, waiting for transfers between devices, on_device(): lax.all_to_all(spread, 'row', 0, 0, tiled=True, axis_index_groups=Z_GROUPS)  8.21 us
    ppermute x2, waiting for transfers between devices, on_device(): lax.ppermute(part, 'depth', [(0, 1), (1, 0)])  7.73 us
    ppermute x2, starting transfers between devices, x_swap(): return lax.ppermute(block, 'row', X_SWAP)  7.32 us
    ppermute x2, waiting for transfers between devices, x_swap(): return lax.ppermute(block, 'row', X_SWAP)  6.36 us
    ppermute x2, starting transfers between devices, on_device(): lax.ppermute(part, 'depth', [(0, 1), (1, 0)])  6.22 us
  transfers between devices with their start and end apart: 13, of which 5 were waited for; matrix products, arithmetic and copies ran while one was open for 5% of the time, Pallas kernels for 14%

profile of v4, /device:TPU:56, one launch (start us, length us, event | category | flops | bytes accessed | tf_op | source)
XLA Modules:
  0.0 132.5 jit_solution(7150881551395545265)
XLA Ops:
  0.6 0.0 copy-start
  0.6 0.9 copy-done
  1.6 1.3 spread_context.1
  2.9 0.0 copy-start.1
  2.9 10.4 %all-to-all-start = ((bf16[8,128,768]{2,1,0:T(8,128)(2,1)}), bf16[8,128,768]{2,1,0:T(8,128)(2,1)}, u32[]{:S(2)}, u32[]{:S(2)}) async-start(bf16[8,128,768]{2,1,0:T(8,128)(2,1)} %spread_context.1), calls=%async_computation | async-start | bytes 3145728 | tf_op jit(solution)/shard_map/all_to_all | solution.py:172
  13.3 0.0 copy-done.1
  13.3 0.2 scale_block.1
  13.5 26.1 %all-gather.1 = f16[2304,768]{1,0:T(8,128)(2,1)S(1)} all-gather(f16[144,768]{1,0:T(8,128)(2,1)S(1)} %convert_element_type.61), channel_id=1, replica_groups=mesh['depth'=2,'row'=16,'col'=16] {'col'}, dimensions={0}, use_global_device_ids=true | all-gather | bytes 3760128 | tf_op jit(solution)/shard_map/all_gather | solution.py:51
  39.6 0.0 copy-start.2
  39.6 2.3 %collective-permute-start = (bf16[768,768]{1,0:T(8,128)(2,1)}, bf16[768,768]{1,0:T(8,128)(2,1)}, u32[]{:S(2)}, u32[]{:S(2)}) collective-permute-start(bf16[768,768]{1,0:T(8,128)(2,1)} %weight.1), channel_id=1, source_target_pairs={{0,1},{1,0},{2,3},{3,2},{4,5},{5,4},{6,7},{7,6},{8,9},{9,8},{10,11... | collective-permute-start | bytes 3538952 | tf_op jit(solution)/shard_map/ppermute | solution.py:62
  42.0 0.0 copy-done.2
  42.0 0.2 fusion.15
  42.2 2.9 %multiply_convert_fusion.grad.here.there.far.partner = bf16[16,128,768]{2,1,0:T(8,128)(2,1)S(1)} fusion(f16[16,144,768]{2,1,0:T(8,128)(2,1)} %bitcast.25, f32[16]{0:T(128)S(1)} %fusion.15), kind=kLoop, calls=%fused_computation | loop fusion | flops 4718592 | bytes 6291520 | tf_op jit(solution)/shard_map/convert_element_type | solution.py:58
  45.2 8.2 %all-to-all-done.context.near = bf16[8,128,768]{2,1,0:T(8,128)(2,1)} async-done(((bf16[8,128,768]{2,1,0:T(8,128)(2,1)}), bf16[8,128,768]{2,1,0:T(8,128)(2,1)}, u32[]{:S(2)}, u32[]{:S(2)}) %all-to-all-start) | async-done | bytes 1572896 | tf_op jit(solution)/shard_map/all_to_all | solution.py:172
  53.4 2.1 %slice.29 = bf16[8,128,384]{2,1,0:T(8,128)(2,1)} slice(bf16[8,128,768]{2,1,0:T(8,128)(2,1)} %all-to-all-done.context.near), slice={[0:8], [0:128], [0:384]} | slice | bytes 1572864 | tf_op jit(solution)/shard_map/slice | solution.py:177
  55.5 4.9 %collective-permute-start.4 = (bf16[8,128,384]{2,1,0:T(8,128)(2,1)}, bf16[8,128,384]{2,1,0:T(8,128)(2,1)}, u32[]{:S(2)}, u32[]{:S(2)}) collective-permute-start(bf16[8,128,384]{2,1,0:T(8,128)(2,1)} %slice.29), channel_id=1, source_target_pairs={{0,128},{16,144},{32,160},{48,176},{64,192},{80,208},{96,224},{112... | collective-permute-start | bytes 2359304 | tf_op jit(solution)/shard_map/ppermute | solution.py:66
  60.4 0.1 pad_add_fusion.places
  60.5 0.0 collective-permute-done.other_weight
  60.5 4.5 %first_products.1 = (bf16[2,128,1536]{2,1,0:T(8,128)(2,1)}, bf16[128,1536]{1,0:T(8,128)(2,1)}, bf16[128,768]{1,0:T(8,128)(2,1)S(1)}) custom-call(s32[4]{0:T(128)S(1)} %pad_add_fusion.places, bf16[16,128,768]{2,1,0:T(8,128)(2,1)S(1)} %multiply_convert_fusion.grad.here.there.far.partner, ...), custom_call_target="tpu_custom_call" | custom-call | flops 1056964608 | bytes 8388608 | tf_op jit(solution)/shard_map/first_products/pallas_call | solution.py:190
  65.0 2.5 %collective-permute-start.2 = (bf16[2,128,1536]{2,1,0:T(8,128)(2,1)}, bf16[2,128,1536]{2,1,0:T(8,128)(2,1)}, u32[]{:S(2)}, u32[]{:S(2)}) collective-permute-start(bf16[2,128,1536]{2,1,0:T(8,128)(2,1)} %get-tuple-element.38), channel_id=1, source_target_pairs={{0,16},{1,113},{2,18},{3,115},{4,20},{5,117},{6,22},{7,119},{8,24}... | collective-permute-start | bytes 2359304 | tf_op jit(solution)/shard_map/ppermute | solution.py:78
  67.5 2.4 %pack_last.1 = bf16[10,128,384]{2,1,0:T(8,128)(2,1)} custom-call(bf16[8,128,768]{2,1,0:T(8,128)(2,1)} %all-to-all-done.context.near, bf16[128,768]{1,0:T(8,128)(2,1)S(1)} %get-tuple-element.34.partner), custom_call_target="tpu_custom_call" | custom-call | bytes 8388608 | tf_op jit(solution)/shard_map/pack_last/pallas_call | solution.py:208
  69.9 2.4 %collective-permute-start.1 = (bf16[10,128,384]{2,1,0:T(8,128)(2,1)}, bf16[10,128,384]{2,1,0:T(8,128)(2,1)}, u32[]{:S(2)}, u32[]{:S(2)}) collective-permute-start(bf16[10,128,384]{2,1,0:T(8,128)(2,1)} %pack_last.1), channel_id=1, source_target_pairs={{0,128},{16,144},{32,160},{48,176},{64,192},{80,208},{96,224},{112... | collective-permute-start | bytes 2949128 | tf_op jit(solution)/shard_map/ppermute | solution.py:66
  72.3 1.9 %collective-permute-start.3 = (bf16[128,1536]{1,0:T(8,128)(2,1)}, bf16[128,1536]{1,0:T(8,128)(2,1)S(1)}, u32[]{:S(2)}, u32[]{:S(2)}) collective-permute-start(bf16[128,1536]{1,0:T(8,128)(2,1)} %get-tuple-element.39), channel_id=1, source_target_pairs={{0,32},{1,97},{2,34},{3,99},{4,36},{5,101},{6,38},{7,103},{8,40},{... | collective-permute-start | bytes 1179656 | tf_op jit(solution)/shard_map/ppermute | solution.py:78
  74.3 0.1 stack.38.places
  74.4 3.4 %near_products.1 = (bf16[2,128,1536]{2,1,0:T(8,128)(2,1)S(1)}, bf16[2,128,1536]{2,1,0:T(8,128)(2,1)S(1)}, bf16[128,768]{1,0:T(8,128)(2,1)S(1)}) custom-call(s32[5]{0:T(128)S(1)} %stack.38.places, bf16[16,128,768]{2,1,0:T(8,128)(2,1)S(1)} %multiply_convert_fusion.grad.here.there.far.partner, bf16[768,768]{1,0:T(8,128)(2,1)} %weight.1, ...), custom_call_target="tpu_custom_call" | custom-call | flops 1358954496 | bytes 8388608 | tf_op jit(solution)/shard_map/near_products/pallas_call | solution.py:219
  77.8 1.9 %collective-permute-done.4.across = bf16[8,128,384]{2,1,0:T(8,128)(2,1)} collective-permute-done((bf16[8,128,384]{2,1,0:T(8,128)(2,1)}, bf16[8,128,384]{2,1,0:T(8,128)(2,1)}, u32[]{:S(2)}, u32[]{:S(2)}) %collective-permute-start.4) | collective-permute-done | bytes 786464 | tf_op jit(solution)/shard_map/ppermute | solution.py:66
  79.7 3.0 %weight_sum.2 = bf16[384,768]{1,0:T(8,128)(2,1)S(1)} custom-call(s32[1]{0:T(128)} %bitcast.13.x_hi, bf16[8,128,768]{2,1,0:T(8,128)(2,1)} %all-to-all-done.context.near, bf16[8,128,384]{2,1,0:T(8,128)(2,1)} %collective-permute-done.4.across, bf16[16,128,768]{2,1,0:T(8,128)(2,1)S(1)} %multiply_convert_fusion.grad.here.there.far.partner), custom_call_target="tpu_custom_call" | custom-call | flops 1207959552 | bytes 8388608 | tf_op jit(solution)/shard_map/weight_sum/pallas_call | solution.py:236
  82.7 5.9 %collective-permute-done.3.far = bf16[128,1536]{1,0:T(8,128)(2,1)S(1)} collective-permute-done((bf16[128,1536]{1,0:T(8,128)(2,1)}, bf16[128,1536]{1,0:T(8,128)(2,1)S(1)}, u32[]{:S(2)}, u32[]{:S(2)}) %collective-permute-start.3) | collective-permute-done | bytes 393248 | tf_op jit(solution)/shard_map/ppermute | solution.py:78
  88.6 0.0 collective-permute-done.2.arrived
  88.6 1.4 %join_sums.1 = bf16[2,128,1536]{2,1,0:T(8,128)(2,1)S(1)} custom-call(s32[1]{0:T(128)} %bitcast.12.at, bf16[2,128,1536]{2,1,0:T(8,128)(2,1)S(1)} %get-tuple-element.37.part, bf16[2,128,1536]{2,1,0:T(8,128)(2,1)} %collective-permute-done.2.arrived, bf16[128,1536]{1,0:T(8,128)(2,1)S(1)} %collective-permute-done.3.far), custom_call_target="tpu_custom_call" | custom-call | bytes 8388608 | tf_op jit(solution)/shard_map/join_sums/pallas_call | solution.py:248
  90.0 3.5 %collective-permute-start.5 = (bf16[2,128,1536]{2,1,0:T(8,128)(2,1)S(1)}, bf16[2,128,1536]{2,1,0:T(8,128)(2,1)S(1)}, u32[]{:S(2)}, u32[]{:S(2)}) collective-permute-start(bf16[2,128,1536]{2,1,0:T(8,128)(2,1)S(1)} %join_sums.1), channel_id=1, source_target_pairs={{0,16},{1,113},{2,18},{3,115},{4,20},{5,117},{6,22},{7,119},{8,24}... | collective-permute-start | bytes 2359304 | tf_op jit(solution)/shard_map/ppermute | solution.py:78
  93.5 1.9 %collective-permute-start.11 = (bf16[384,768]{1,0:T(8,128)(2,1)S(1)}, bf16[384,768]{1,0:T(8,128)(2,1)S(1)}, u32[]{:S(2)}, u32[]{:S(2)}) collective-permute-start(bf16[384,768]{1,0:T(8,128)(2,1)S(1)} %weight_sum.2), channel_id=1, source_target_pairs={{0,256},{256,0},{1,257},{257,1},{2,258},{258,2},{3,259},{259,3},{4... | collective-permute-start | bytes 1769480 | tf_op jit(solution)/shard_map/ppermute | solution.py:245
  95.4 4.5 %collective-permute-done.1.across = bf16[10,128,384]{2,1,0:T(8,128)(2,1)} collective-permute-done((bf16[10,128,384]{2,1,0:T(8,128)(2,1)}, bf16[10,128,384]{2,1,0:T(8,128)(2,1)}, u32[]{:S(2)}, u32[]{:S(2)}) %collective-permute-start.1) | collective-permute-done | bytes 983072 | tf_op jit(solution)/shard_map/ppermute | solution.py:66
  99.8 3.1 %weight_sum.3 = bf16[384,768]{1,0:T(8,128)(2,1)S(1)} custom-call(s32[1]{0:T(128)} %bitcast.13.x_hi, bf16[8,128,768]{2,1,0:T(8,128)(2,1)} %all-to-all-done.context.near, bf16[10,128,384]{2,1,0:T(8,128)(2,1)} %collective-permute-done.1.across, bf16[16,128,768]{2,1,0:T(8,128)(2,1)S(1)} %multiply_convert_fusion.grad.here.there.far.partner), custom_call_target="tpu_custom_call" | custom-call | flops 1207959552 | bytes 8388608 | tf_op jit(solution)/shard_map/weight_sum/pallas_call | solution.py:236
  102.9 4.3 %collective-permute-start.10 = (bf16[384,768]{1,0:T(8,128)(2,1)S(1)}, bf16[384,768]{1,0:T(8,128)(2,1)S(1)}, u32[]{:S(2)}, u32[]{:S(2)}) collective-permute-start(bf16[384,768]{1,0:T(8,128)(2,1)S(1)} %weight_sum.3), channel_id=1, source_target_pairs={{0,256},{256,0},{1,257},{257,1},{2,258},{258,2},{3,259},{259,3},{4... | collective-permute-start | bytes 1769480 | tf_op jit(solution)/shard_map/ppermute | solution.py:245
  107.2 1.0 slice_bitcast_fusion.5
  108.2 0.0 collective-permute-done.5
  108.2 0.2 add_convert_fusion
  108.4 0.1 slice_bitcast_fusion
  108.5 2.4 %collective-permute-start.6 = (bf16[128,768]{1,0:T(8,128)(2,1)S(1)}, bf16[128,768]{1,0:T(8,128)(2,1)S(1)}, u32[]{:S(2)}, u32[]{:S(2)}) collective-permute-start(bf16[128,768]{1,0:T(8,128)(2,1)S(1)} %get-tuple-element.57), channel_id=1, source_target_pairs={{0,16},{1,113},{2,18},{3,115},{4,20},{5,117},{6,22},{7,119},{8,24}... | collective-permute-start | bytes 589832 | tf_op jit(solution)/shard_map/ppermute | solution.py:78
  110.9 1.9 %collective-permute-start.7 = (bf16[128,768]{1,0:T(8,128)(2,1)S(1)}, bf16[128,768]{1,0:T(8,128)(2,1)S(1)}, u32[]{:S(2)}, u32[]{:S(2)}) collective-permute-start(bf16[128,768]{1,0:T(8,128)(2,1)S(1)} %get-tuple-element.56), channel_id=1, source_target_pairs={{0,17},{1,112},{2,19},{3,114},{4,21},{5,116},{6,23},{7,118},{8,25}... | collective-permute-start | bytes 589832 | tf_op jit(solution)/shard_map/ppermute | solution.py:78
  112.8 4.7 %collective-permute-start.8 = (bf16[128,768]{1,0:T(8,128)(2,1)S(1)}, bf16[128,768]{1,0:T(8,128)(2,1)S(1)}, u32[]{:S(2)}, u32[]{:S(2)}) collective-permute-start(bf16[128,768]{1,0:T(8,128)(2,1)S(1)} %get-tuple-element.55), channel_id=1, source_target_pairs={{0,144},{1,241},{2,146},{3,243},{4,148},{5,245},{6,150},{7,247},{8... | collective-permute-start | bytes 589832 | tf_op jit(solution)/shard_map/ppermute | solution.py:78
  117.5 0.0 collective-permute-done.11
  117.5 5.7 %collective-permute-start.9 = (bf16[128,768]{1,0:T(8,128)(2,1)S(1)}, bf16[128,768]{1,0:T(8,128)(2,1)S(1)}, u32[]{:S(2)}, u32[]{:S(2)}) collective-permute-start(bf16[128,768]{1,0:T(8,128)(2,1)S(1)} %get-tuple-element.54), channel_id=1, source_target_pairs={{0,145},{1,240},{2,147},{3,242},{4,149},{5,244},{6,151},{7,246},{8... | collective-permute-start | bytes 589832 | tf_op jit(solution)/shard_map/ppermute | solution.py:78
  123.3 0.1 add_convert_fusion.2
  123.4 0.1 dynamic_update_slice.6
  123.5 7.7 %collective-permute-done.10 = bf16[384,768]{1,0:T(8,128)(2,1)S(1)} collective-permute-done((bf16[384,768]{1,0:T(8,128)(2,1)S(1)}, bf16[384,768]{1,0:T(8,128)(2,1)S(1)}, u32[]{:S(2)}, u32[]{:S(2)}) %collective-permute-start.10) | collective-permute-done | bytes 589856 | tf_op jit(solution)/shard_map/ppermute | solution.py:245
  131.2 0.0 collective-permute-done.6
  131.2 0.0 collective-permute-done.7
  131.3 0.0 collective-permute-done.8
  131.3 0.0 collective-permute-done.9
  131.3 0.1 fusion
  131.4 0.0 copy-start.3
  131.4 1.0 add_convert_fusion.3
  132.5 0.0 copy-done.3
  (2 shorter events, 0.1 us)
Async XLA Ops:
  0.6 0.9 copy-start
  2.9 10.5 %copy-start.1 = (bf16[128,768]{1,0:T(8,128)(2,1)S(1)}, bf16[128,768]{1,0:T(8,128)(2,1)}, u32[]{:S(2)}) copy-start(bf16[128,768]{1,0:T(8,128)(2,1)} %block.2) | copy-start | bytes 589828
  2.9 50.5 %all-to-all-start = ((bf16[8,128,768]{2,1,0:T(8,128)(2,1)}), bf16[8,128,768]{2,1,0:T(8,128)(2,1)}, u32[]{:S(2)}, u32[]{:S(2)}) async-start(bf16[8,128,768]{2,1,0:T(8,128)(2,1)} %spread_context.1), calls=%async_computation | async-start | bytes 3145728 | tf_op jit(solution)/shard_map/all_to_all | solution.py:172
  39.6 2.4 %copy-start.2 = (f16[2304,768]{1,0:T(8,128)(2,1)}, f16[2304,768]{1,0:T(8,128)(2,1)S(1)}, u32[]{:S(2)}) copy-start(f16[2304,768]{1,0:T(8,128)(2,1)S(1)} %all-gather.1) | copy-start | bytes 10616836
  39.6 20.9 %collective-permute-start = (bf16[768,768]{1,0:T(8,128)(2,1)}, bf16[768,768]{1,0:T(8,128)(2,1)}, u32[]{:S(2)}, u32[]{:S(2)}) collective-permute-start(bf16[768,768]{1,0:T(8,128)(2,1)} %weight.1), channel_id=1, source_target_pairs={{0,1},{1,0},{2,3},{3,2},{4,5},{5,4},{6,7},{7,6},{8,9},{9,8},{10,11... | collective-permute-start | bytes 3538952 | tf_op jit(solution)/shard_map/ppermute | solution.py:62
  55.5 24.2 %collective-permute-start.4 = (bf16[8,128,384]{2,1,0:T(8,128)(2,1)}, bf16[8,128,384]{2,1,0:T(8,128)(2,1)}, u32[]{:S(2)}, u32[]{:S(2)}) collective-permute-start(bf16[8,128,384]{2,1,0:T(8,128)(2,1)} %slice.29), channel_id=1, source_target_pairs={{0,128},{16,144},{32,160},{48,176},{64,192},{80,208},{96,224},{112... | collective-permute-start | bytes 2359304 | tf_op jit(solution)/shard_map/ppermute | solution.py:66
  65.0 23.6 %collective-permute-start.2 = (bf16[2,128,1536]{2,1,0:T(8,128)(2,1)}, bf16[2,128,1536]{2,1,0:T(8,128)(2,1)}, u32[]{:S(2)}, u32[]{:S(2)}) collective-permute-start(bf16[2,128,1536]{2,1,0:T(8,128)(2,1)} %get-tuple-element.38), channel_id=1, source_target_pairs={{0,16},{1,113},{2,18},{3,115},{4,20},{5,117},{6,22},{7,119},{8,24}... | collective-permute-start | bytes 2359304 | tf_op jit(solution)/shard_map/ppermute | solution.py:78
  69.9 29.9 %collective-permute-start.1 = (bf16[10,128,384]{2,1,0:T(8,128)(2,1)}, bf16[10,128,384]{2,1,0:T(8,128)(2,1)}, u32[]{:S(2)}, u32[]{:S(2)}) collective-permute-start(bf16[10,128,384]{2,1,0:T(8,128)(2,1)} %pack_last.1), channel_id=1, source_target_pairs={{0,128},{16,144},{32,160},{48,176},{64,192},{80,208},{96,224},{112... | collective-permute-start | bytes 2949128 | tf_op jit(solution)/shard_map/ppermute | solution.py:66
  72.3 16.3 %collective-permute-start.3 = (bf16[128,1536]{1,0:T(8,128)(2,1)}, bf16[128,1536]{1,0:T(8,128)(2,1)S(1)}, u32[]{:S(2)}, u32[]{:S(2)}) collective-permute-start(bf16[128,1536]{1,0:T(8,128)(2,1)} %get-tuple-element.39), channel_id=1, source_target_pairs={{0,32},{1,97},{2,34},{3,99},{4,36},{5,101},{6,38},{7,103},{8,40},{... | collective-permute-start | bytes 1179656 | tf_op jit(solution)/shard_map/ppermute | solution.py:78
  90.0 18.3 %collective-permute-start.5 = (bf16[2,128,1536]{2,1,0:T(8,128)(2,1)S(1)}, bf16[2,128,1536]{2,1,0:T(8,128)(2,1)S(1)}, u32[]{:S(2)}, u32[]{:S(2)}) collective-permute-start(bf16[2,128,1536]{2,1,0:T(8,128)(2,1)S(1)} %join_sums.1), channel_id=1, source_target_pairs={{0,16},{1,113},{2,18},{3,115},{4,20},{5,117},{6,22},{7,119},{8,24}... | collective-permute-start | bytes 2359304 | tf_op jit(solution)/shard_map/ppermute | solution.py:78
  93.5 24.1 %collective-permute-start.11 = (bf16[384,768]{1,0:T(8,128)(2,1)S(1)}, bf16[384,768]{1,0:T(8,128)(2,1)S(1)}, u32[]{:S(2)}, u32[]{:S(2)}) collective-permute-start(bf16[384,768]{1,0:T(8,128)(2,1)S(1)} %weight_sum.2), channel_id=1, source_target_pairs={{0,256},{256,0},{1,257},{257,1},{2,258},{258,2},{3,259},{259,3},{4... | collective-permute-start | bytes 1769480 | tf_op jit(solution)/shard_map/ppermute | solution.py:245
  102.9 28.3 %collective-permute-start.10 = (bf16[384,768]{1,0:T(8,128)(2,1)S(1)}, bf16[384,768]{1,0:T(8,128)(2,1)S(1)}, u32[]{:S(2)}, u32[]{:S(2)}) collective-permute-start(bf16[384,768]{1,0:T(8,128)(2,1)S(1)} %weight_sum.3), channel_id=1, source_target_pairs={{0,256},{256,0},{1,257},{257,1},{2,258},{258,2},{3,259},{259,3},{4... | collective-permute-start | bytes 1769480 | tf_op jit(solution)/shard_map/ppermute | solution.py:245
  108.5 22.7 %collective-permute-start.6 = (bf16[128,768]{1,0:T(8,128)(2,1)S(1)}, bf16[128,768]{1,0:T(8,128)(2,1)S(1)}, u32[]{:S(2)}, u32[]{:S(2)}) collective-permute-start(bf16[128,768]{1,0:T(8,128)(2,1)S(1)} %get-tuple-element.57), channel_id=1, source_target_pairs={{0,16},{1,113},{2,18},{3,115},{4,20},{5,117},{6,22},{7,119},{8,24}... | collective-permute-start | bytes 589832 | tf_op jit(solution)/shard_map/ppermute | solution.py:78
  110.9 20.4 %collective-permute-start.7 = (bf16[128,768]{1,0:T(8,128)(2,1)S(1)}, bf16[128,768]{1,0:T(8,128)(2,1)S(1)}, u32[]{:S(2)}, u32[]{:S(2)}) collective-permute-start(bf16[128,768]{1,0:T(8,128)(2,1)S(1)} %get-tuple-element.56), channel_id=1, source_target_pairs={{0,17},{1,112},{2,19},{3,114},{4,21},{5,116},{6,23},{7,118},{8,25}... | collective-permute-start | bytes 589832 | tf_op jit(solution)/shard_map/ppermute | solution.py:78
  112.8 18.5 %collective-permute-start.8 = (bf16[128,768]{1,0:T(8,128)(2,1)S(1)}, bf16[128,768]{1,0:T(8,128)(2,1)S(1)}, u32[]{:S(2)}, u32[]{:S(2)}) collective-permute-start(bf16[128,768]{1,0:T(8,128)(2,1)S(1)} %get-tuple-element.55), channel_id=1, source_target_pairs={{0,144},{1,241},{2,146},{3,243},{4,148},{5,245},{6,150},{7,247},{8... | collective-permute-start | bytes 589832 | tf_op jit(solution)/shard_map/ppermute | solution.py:78
  117.5 13.7 %collective-permute-start.9 = (bf16[128,768]{1,0:T(8,128)(2,1)S(1)}, bf16[128,768]{1,0:T(8,128)(2,1)S(1)}, u32[]{:S(2)}, u32[]{:S(2)}) collective-permute-start(bf16[128,768]{1,0:T(8,128)(2,1)S(1)} %get-tuple-element.54), channel_id=1, source_target_pairs={{0,145},{1,240},{2,147},{3,242},{4,149},{5,244},{6,151},{7,246},{8... | collective-permute-start | bytes 589832 | tf_op jit(solution)/shard_map/ppermute | solution.py:78
  131.4 1.1 copy-start.3

commit v5 on v4

--- a/solution.py
+++ b/solution.py
@@ -113,7 +113,7 @@
 
 def last_kernel(context, partner, out):
     part = out.shape[2]
-    out[:Z] = context[:, :, -part:]
+    out[:Z] = context[...]
     for i in range(PARTS):
         out[Z + i] = partner[:, i * part : (i + 1) * part]
 
@@ -209,8 +209,12 @@
         last_kernel,
         [(Z + PARTS, rows, part)],
         0,
-        in_specs=[IN_VMEM] * 2,
-        out_specs=[IN_VMEM],
+        grid=(1,),
+        in_specs=[
+            pl.BlockSpec((Z, rows, part), lambda i: (0, 0, PARTS - 1)),
+            pl.BlockSpec((rows, width), lambda i: (0, 0)),
+        ],
+        out_specs=[pl.BlockSpec((Z + PARTS, rows, part), lambda i: (0, 0, 0))],
         name="pack_last",
     )(near, partner)
     far, packed = together((far, packed))

time: 133 us -> 133 us (level)
  transfers between devices with their start and end apart: 13 -> 13, of which waited for: 5 -> 5; matrix products, arithmetic and copies ran while one was open for 5% -> 5% of each run, Pallas kernels for 14% -> 13%
where the time goes in v5:
time: 133 us; the launch traced here: 132 us
  starting transfers between devices  49 us (37%)
  waiting for transfers between devices  28.3 us (21%)
  blocking collectives  26.1 us (20%)
  Pallas kernels  19 us (14%)
  other arithmetic  4.82 us (4%)
  local copies, waits for them, and re-layouts  4.25 us (3%)
    all_gather x1, blocking collectives, gather_grad(): return lax.all_gather(sent.astype(F16), 'col', axis=0, tiled=True)  26.1 us
    ppermute x7, starting transfers between devices, ring(): return lax.ppermute(block, ('row', 'col'), pairs)  22.9 us
    all_to_all x1, starting transfers between devices, on_device(): lax.all_to_all(spread, 'row', 0, 0, tiled=True, axis_index_groups=Z_GROUPS)  10.4 us
    all_to_all x1, waiting for transfers between devices, on_device(): lax.all_to_all(spread, 'row', 0, 0, tiled=True, axis_index_groups=Z_GROUPS)  8.21 us
    ppermute x2, waiting for transfers between devices, on_device(): lax.ppermute(part, 'depth', [(0, 1), (1, 0)])  7.73 us
    ppermute x2, starting transfers between devices, x_swap(): return lax.ppermute(block, 'row', X_SWAP)  7.32 us
    ppermute x2, waiting for transfers between devices, x_swap(): return lax.ppermute(block, 'row', X_SWAP)  6.72 us
    ppermute x2, starting transfers between devices, on_device(): lax.ppermute(part, 'depth', [(0, 1), (1, 0)])  6.14 us
  transfers between devices with their start and end apart: 13, of which 5 were waited for; matrix products, arithmetic and copies ran while one was open for 5% of the time, Pallas kernels for 13%

profile of v5, /device:TPU:56, one launch (start us, length us, event | category | flops | bytes accessed | tf_op | source)
XLA Modules:
  0.0 132.5 jit_solution(16817851109950537341)
XLA Ops:
  0.6 0.0 copy-start
  0.6 0.9 copy-done
  1.6 1.3 spread_context.1
  2.9 0.0 copy-start.1
  2.9 10.4 %all-to-all-start = ((bf16[8,128,768]{2,1,0:T(8,128)(2,1)}), bf16[8,128,768]{2,1,0:T(8,128)(2,1)}, u32[]{:S(2)}, u32[]{:S(2)}) async-start(bf16[8,128,768]{2,1,0:T(8,128)(2,1)} %spread_context.1), calls=%async_computation | async-start | bytes 3145728 | tf_op jit(solution)/shard_map/all_to_all | solution.py:172
  13.3 0.0 copy-done.1
  13.3 0.2 scale_block.1
  13.5 26.1 %all-gather.1 = f16[2304,768]{1,0:T(8,128)(2,1)S(1)} all-gather(f16[144,768]{1,0:T(8,128)(2,1)S(1)} %convert_element_type.61), channel_id=1, replica_groups=mesh['depth'=2,'row'=16,'col'=16] {'col'}, dimensions={0}, use_global_device_ids=true | all-gather | bytes 3760128 | tf_op jit(solution)/shard_map/all_gather | solution.py:51
  39.6 0.0 copy-start.2
  39.6 2.3 %collective-permute-start = (bf16[768,768]{1,0:T(8,128)(2,1)}, bf16[768,768]{1,0:T(8,128)(2,1)}, u32[]{:S(2)}, u32[]{:S(2)}) collective-permute-start(bf16[768,768]{1,0:T(8,128)(2,1)} %weight.1), channel_id=1, source_target_pairs={{0,1},{1,0},{2,3},{3,2},{4,5},{5,4},{6,7},{7,6},{8,9},{9,8},{10,11... | collective-permute-start | bytes 3538952 | tf_op jit(solution)/shard_map/ppermute | solution.py:62
  42.0 0.0 copy-done.2
  42.0 0.2 fusion.15
  42.2 2.9 %multiply_convert_fusion.grad.here.there.far.partner = bf16[16,128,768]{2,1,0:T(8,128)(2,1)S(1)} fusion(f16[16,144,768]{2,1,0:T(8,128)(2,1)} %bitcast.25, f32[16]{0:T(128)S(1)} %fusion.15), kind=kLoop, calls=%fused_computation | loop fusion | flops 4718592 | bytes 6291520 | tf_op jit(solution)/shard_map/convert_element_type | solution.py:58
  45.2 8.2 %all-to-all-done.context.near = bf16[8,128,768]{2,1,0:T(8,128)(2,1)} async-done(((bf16[8,128,768]{2,1,0:T(8,128)(2,1)}), bf16[8,128,768]{2,1,0:T(8,128)(2,1)}, u32[]{:S(2)}, u32[]{:S(2)}) %all-to-all-start) | async-done | bytes 1572896 | tf_op jit(solution)/shard_map/all_to_all | solution.py:172
  53.4 2.1 %slice.29 = bf16[8,128,384]{2,1,0:T(8,128)(2,1)} slice(bf16[8,128,768]{2,1,0:T(8,128)(2,1)} %all-to-all-done.context.near), slice={[0:8], [0:128], [0:384]} | slice | bytes 1572864 | tf_op jit(solution)/shard_map/slice | solution.py:177
  55.5 4.9 %collective-permute-start.4 = (bf16[8,128,384]{2,1,0:T(8,128)(2,1)}, bf16[8,128,384]{2,1,0:T(8,128)(2,1)}, u32[]{:S(2)}, u32[]{:S(2)}) collective-permute-start(bf16[8,128,384]{2,1,0:T(8,128)(2,1)} %slice.29), channel_id=1, source_target_pairs={{0,128},{16,144},{32,160},{48,176},{64,192},{80,208},{96,224},{112... | collective-permute-start | bytes 2359304 | tf_op jit(solution)/shard_map/ppermute | solution.py:66
  60.4 0.1 pad_add_fusion.places
  60.5 0.0 collective-permute-done.other_weight
  60.5 4.5 %first_products.1 = (bf16[2,128,1536]{2,1,0:T(8,128)(2,1)}, bf16[128,1536]{1,0:T(8,128)(2,1)}, bf16[128,768]{1,0:T(8,128)(2,1)S(1)}) custom-call(s32[4]{0:T(128)S(1)} %pad_add_fusion.places, bf16[16,128,768]{2,1,0:T(8,128)(2,1)S(1)} %multiply_convert_fusion.grad.here.there.far.partner, ...), custom_call_target="tpu_custom_call" | custom-call | flops 1056964608 | bytes 8388608 | tf_op jit(solution)/shard_map/first_products/pallas_call | solution.py:190
  65.0 2.5 %collective-permute-start.2 = (bf16[2,128,1536]{2,1,0:T(8,128)(2,1)}, bf16[2,128,1536]{2,1,0:T(8,128)(2,1)}, u32[]{:S(2)}, u32[]{:S(2)}) collective-permute-start(bf16[2,128,1536]{2,1,0:T(8,128)(2,1)} %get-tuple-element.38), channel_id=1, source_target_pairs={{0,16},{1,113},{2,18},{3,115},{4,20},{5,117},{6,22},{7,119},{8,24}... | collective-permute-start | bytes 2359304 | tf_op jit(solution)/shard_map/ppermute | solution.py:78
  67.5 2.2 %pack_last.1 = bf16[10,128,384]{2,1,0:T(8,128)(2,1)} custom-call(bf16[8,128,768]{2,1,0:T(8,128)(2,1)} %all-to-all-done.context.near, bf16[128,768]{1,0:T(8,128)(2,1)S(1)} %get-tuple-element.34.partner), custom_call_target="tpu_custom_call" | custom-call | bytes 8388608 | tf_op jit(solution)/shard_map/pack_last/pallas_call | solution.py:208
  69.6 2.4 %collective-permute-start.1 = (bf16[10,128,384]{2,1,0:T(8,128)(2,1)}, bf16[10,128,384]{2,1,0:T(8,128)(2,1)}, u32[]{:S(2)}, u32[]{:S(2)}) collective-permute-start(bf16[10,128,384]{2,1,0:T(8,128)(2,1)} %pack_last.1), channel_id=1, source_target_pairs={{0,128},{16,144},{32,160},{48,176},{64,192},{80,208},{96,224},{112... | collective-permute-start | bytes 2949128 | tf_op jit(solution)/shard_map/ppermute | solution.py:66
  72.0 1.9 %collective-permute-start.3 = (bf16[128,1536]{1,0:T(8,128)(2,1)}, bf16[128,1536]{1,0:T(8,128)(2,1)S(1)}, u32[]{:S(2)}, u32[]{:S(2)}) collective-permute-start(bf16[128,1536]{1,0:T(8,128)(2,1)} %get-tuple-element.39), channel_id=1, source_target_pairs={{0,32},{1,97},{2,34},{3,99},{4,36},{5,101},{6,38},{7,103},{8,40},{... | collective-permute-start | bytes 1179656 | tf_op jit(solution)/shard_map/ppermute | solution.py:78
  74.0 0.1 stack.38.places
  74.1 3.4 %near_products.1 = (bf16[2,128,1536]{2,1,0:T(8,128)(2,1)S(1)}, bf16[2,128,1536]{2,1,0:T(8,128)(2,1)S(1)}, bf16[128,768]{1,0:T(8,128)(2,1)S(1)}) custom-call(s32[5]{0:T(128)S(1)} %stack.38.places, bf16[16,128,768]{2,1,0:T(8,128)(2,1)S(1)} %multiply_convert_fusion.grad.here.there.far.partner, bf16[768,768]{1,0:T(8,128)(2,1)} %weight.1, ...), custom_call_target="tpu_custom_call" | custom-call | flops 1358954496 | bytes 8388608 | tf_op jit(solution)/shard_map/near_products/pallas_call | solution.py:223
  77.5 2.2 %collective-permute-done.4.across = bf16[8,128,384]{2,1,0:T(8,128)(2,1)} collective-permute-done((bf16[8,128,384]{2,1,0:T(8,128)(2,1)}, bf16[8,128,384]{2,1,0:T(8,128)(2,1)}, u32[]{:S(2)}, u32[]{:S(2)}) %collective-permute-start.4) | collective-permute-done | bytes 786464 | tf_op jit(solution)/shard_map/ppermute | solution.py:66
  79.7 3.0 %weight_sum.2 = bf16[384,768]{1,0:T(8,128)(2,1)S(1)} custom-call(s32[1]{0:T(128)} %bitcast.13.x_hi, bf16[8,128,768]{2,1,0:T(8,128)(2,1)} %all-to-all-done.context.near, bf16[8,128,384]{2,1,0:T(8,128)(2,1)} %collective-permute-done.4.across, bf16[16,128,768]{2,1,0:T(8,128)(2,1)S(1)} %multiply_convert_fusion.grad.here.there.far.partner), custom_call_target="tpu_custom_call" | custom-call | flops 1207959552 | bytes 8388608 | tf_op jit(solution)/shard_map/weight_sum/pallas_call | solution.py:240
  82.7 5.6 %collective-permute-done.3.far = bf16[128,1536]{1,0:T(8,128)(2,1)S(1)} collective-permute-done((bf16[128,1536]{1,0:T(8,128)(2,1)}, bf16[128,1536]{1,0:T(8,128)(2,1)S(1)}, u32[]{:S(2)}, u32[]{:S(2)}) %collective-permute-start.3) | collective-permute-done | bytes 393248 | tf_op jit(solution)/shard_map/ppermute | solution.py:78
  88.3 0.0 collective-permute-done.2.arrived
  88.3 1.4 %join_sums.1 = bf16[2,128,1536]{2,1,0:T(8,128)(2,1)S(1)} custom-call(s32[1]{0:T(128)} %bitcast.12.at, bf16[2,128,1536]{2,1,0:T(8,128)(2,1)S(1)} %get-tuple-element.37.part, bf16[2,128,1536]{2,1,0:T(8,128)(2,1)} %collective-permute-done.2.arrived, bf16[128,1536]{1,0:T(8,128)(2,1)S(1)} %collective-permute-done.3.far), custom_call_target="tpu_custom_call" | custom-call | bytes 8388608 | tf_op jit(solution)/shard_map/join_sums/pallas_call | solution.py:252
  89.7 3.7 %collective-permute-start.5 = (bf16[2,128,1536]{2,1,0:T(8,128)(2,1)S(1)}, bf16[2,128,1536]{2,1,0:T(8,128)(2,1)S(1)}, u32[]{:S(2)}, u32[]{:S(2)}) collective-permute-start(bf16[2,128,1536]{2,1,0:T(8,128)(2,1)S(1)} %join_sums.1), channel_id=1, source_target_pairs={{0,16},{1,113},{2,18},{3,115},{4,20},{5,117},{6,22},{7,119},{8,24}... | collective-permute-start | bytes 2359304 | tf_op jit(solution)/shard_map/ppermute | solution.py:78
  93.5 1.9 %collective-permute-start.11 = (bf16[384,768]{1,0:T(8,128)(2,1)S(1)}, bf16[384,768]{1,0:T(8,128)(2,1)S(1)}, u32[]{:S(2)}, u32[]{:S(2)}) collective-permute-start(bf16[384,768]{1,0:T(8,128)(2,1)S(1)} %weight_sum.2), channel_id=1, source_target_pairs={{0,256},{256,0},{1,257},{257,1},{2,258},{258,2},{3,259},{259,3},{4... | collective-permute-start | bytes 1769480 | tf_op jit(solution)/shard_map/ppermute | solution.py:249
  95.4 4.5 %collective-permute-done.1.across = bf16[10,128,384]{2,1,0:T(8,128)(2,1)} collective-permute-done((bf16[10,128,384]{2,1,0:T(8,128)(2,1)}, bf16[10,128,384]{2,1,0:T(8,128)(2,1)}, u32[]{:S(2)}, u32[]{:S(2)}) %collective-permute-start.1) | collective-permute-done | bytes 983072 | tf_op jit(solution)/shard_map/ppermute | solution.py:66
  99.9 3.1 %weight_sum.3 = bf16[384,768]{1,0:T(8,128)(2,1)S(1)} custom-call(s32[1]{0:T(128)} %bitcast.13.x_hi, bf16[8,128,768]{2,1,0:T(8,128)(2,1)} %all-to-all-done.context.near, bf16[10,128,384]{2,1,0:T(8,128)(2,1)} %collective-permute-done.1.across, bf16[16,128,768]{2,1,0:T(8,128)(2,1)S(1)} %multiply_convert_fusion.grad.here.there.far.partner), custom_call_target="tpu_custom_call" | custom-call | flops 1207959552 | bytes 8388608 | tf_op jit(solution)/shard_map/weight_sum/pallas_call | solution.py:240
  103.0 4.2 %collective-permute-start.10 = (bf16[384,768]{1,0:T(8,128)(2,1)S(1)}, bf16[384,768]{1,0:T(8,128)(2,1)S(1)}, u32[]{:S(2)}, u32[]{:S(2)}) collective-permute-start(bf16[384,768]{1,0:T(8,128)(2,1)S(1)} %weight_sum.3), channel_id=1, source_target_pairs={{0,256},{256,0},{1,257},{257,1},{2,258},{258,2},{3,259},{259,3},{4... | collective-permute-start | bytes 1769480 | tf_op jit(solution)/shard_map/ppermute | solution.py:249
  107.2 1.0 slice_bitcast_fusion.5
  108.2 0.0 collective-permute-done.5
  108.2 0.2 add_convert_fusion
  108.4 0.1 slice_bitcast_fusion
  108.5 2.5 %collective-permute-start.6 = (bf16[128,768]{1,0:T(8,128)(2,1)S(1)}, bf16[128,768]{1,0:T(8,128)(2,1)S(1)}, u32[]{:S(2)}, u32[]{:S(2)}) collective-permute-start(bf16[128,768]{1,0:T(8,128)(2,1)S(1)} %get-tuple-element.57), channel_id=1, source_target_pairs={{0,16},{1,113},{2,18},{3,115},{4,20},{5,117},{6,22},{7,119},{8,24}... | collective-permute-start | bytes 589832 | tf_op jit(solution)/shard_map/ppermute | solution.py:78
  111.0 1.9 %collective-permute-start.7 = (bf16[128,768]{1,0:T(8,128)(2,1)S(1)}, bf16[128,768]{1,0:T(8,128)(2,1)S(1)}, u32[]{:S(2)}, u32[]{:S(2)}) collective-permute-start(bf16[128,768]{1,0:T(8,128)(2,1)S(1)} %get-tuple-element.56), channel_id=1, source_target_pairs={{0,17},{1,112},{2,19},{3,114},{4,21},{5,116},{6,23},{7,118},{8,25}... | collective-permute-start | bytes 589832 | tf_op jit(solution)/shard_map/ppermute | solution.py:78
  112.9 4.6 %collective-permute-start.8 = (bf16[128,768]{1,0:T(8,128)(2,1)S(1)}, bf16[128,768]{1,0:T(8,128)(2,1)S(1)}, u32[]{:S(2)}, u32[]{:S(2)}) collective-permute-start(bf16[128,768]{1,0:T(8,128)(2,1)S(1)} %get-tuple-element.55), channel_id=1, source_target_pairs={{0,144},{1,241},{2,146},{3,243},{4,148},{5,245},{6,150},{7,247},{8... | collective-permute-start | bytes 589832 | tf_op jit(solution)/shard_map/ppermute | solution.py:78
  117.5 0.0 collective-permute-done.11
  117.5 5.7 %collective-permute-start.9 = (bf16[128,768]{1,0:T(8,128)(2,1)S(1)}, bf16[128,768]{1,0:T(8,128)(2,1)S(1)}, u32[]{:S(2)}, u32[]{:S(2)}) collective-permute-start(bf16[128,768]{1,0:T(8,128)(2,1)S(1)} %get-tuple-element.54), channel_id=1, source_target_pairs={{0,145},{1,240},{2,147},{3,242},{4,149},{5,244},{6,151},{7,246},{8... | collective-permute-start | bytes 589832 | tf_op jit(solution)/shard_map/ppermute | solution.py:78
  123.3 0.1 add_convert_fusion.2
  123.4 0.1 dynamic_update_slice.6
  123.5 7.7 %collective-permute-done.10 = bf16[384,768]{1,0:T(8,128)(2,1)S(1)} collective-permute-done((bf16[384,768]{1,0:T(8,128)(2,1)S(1)}, bf16[384,768]{1,0:T(8,128)(2,1)S(1)}, u32[]{:S(2)}, u32[]{:S(2)}) %collective-permute-start.10) | collective-permute-done | bytes 589856 | tf_op jit(solution)/shard_map/ppermute | solution.py:249
  131.2 0.0 collective-permute-done.6
  131.2 0.0 collective-permute-done.7
  131.3 0.0 collective-permute-done.8
  131.3 0.0 collective-permute-done.9
  131.3 0.1 fusion
  131.4 0.0 copy-start.3
  131.4 1.0 add_convert_fusion.3
  132.5 0.0 copy-done.3
  (2 shorter events, 0.1 us)
Async XLA Ops:
  0.6 0.9 copy-start
  2.9 10.5 %copy-start.1 = (bf16[128,768]{1,0:T(8,128)(2,1)S(1)}, bf16[128,768]{1,0:T(8,128)(2,1)}, u32[]{:S(2)}) copy-start(bf16[128,768]{1,0:T(8,128)(2,1)} %block.2) | copy-start | bytes 589828
  2.9 50.5 %all-to-all-start = ((bf16[8,128,768]{2,1,0:T(8,128)(2,1)}), bf16[8,128,768]{2,1,0:T(8,128)(2,1)}, u32[]{:S(2)}, u32[]{:S(2)}) async-start(bf16[8,128,768]{2,1,0:T(8,128)(2,1)} %spread_context.1), calls=%async_computation | async-start | bytes 3145728 | tf_op jit(solution)/shard_map/all_to_all | solution.py:172
  39.6 2.4 %copy-start.2 = (f16[2304,768]{1,0:T(8,128)(2,1)}, f16[2304,768]{1,0:T(8,128)(2,1)S(1)}, u32[]{:S(2)}) copy-start(f16[2304,768]{1,0:T(8,128)(2,1)S(1)} %all-gather.1) | copy-start | bytes 10616836
  39.6 20.9 %collective-permute-start = (bf16[768,768]{1,0:T(8,128)(2,1)}, bf16[768,768]{1,0:T(8,128)(2,1)}, u32[]{:S(2)}, u32[]{:S(2)}) collective-permute-start(bf16[768,768]{1,0:T(8,128)(2,1)} %weight.1), channel_id=1, source_target_pairs={{0,1},{1,0},{2,3},{3,2},{4,5},{5,4},{6,7},{7,6},{8,9},{9,8},{10,11... | collective-permute-start | bytes 3538952 | tf_op jit(solution)/shard_map/ppermute | solution.py:62
  55.5 24.2 %collective-permute-start.4 = (bf16[8,128,384]{2,1,0:T(8,128)(2,1)}, bf16[8,128,384]{2,1,0:T(8,128)(2,1)}, u32[]{:S(2)}, u32[]{:S(2)}) collective-permute-start(bf16[8,128,384]{2,1,0:T(8,128)(2,1)} %slice.29), channel_id=1, source_target_pairs={{0,128},{16,144},{32,160},{48,176},{64,192},{80,208},{96,224},{112... | collective-permute-start | bytes 2359304 | tf_op jit(solution)/shard_map/ppermute | solution.py:66
  65.0 23.4 %collective-permute-start.2 = (bf16[2,128,1536]{2,1,0:T(8,128)(2,1)}, bf16[2,128,1536]{2,1,0:T(8,128)(2,1)}, u32[]{:S(2)}, u32[]{:S(2)}) collective-permute-start(bf16[2,128,1536]{2,1,0:T(8,128)(2,1)} %get-tuple-element.38), channel_id=1, source_target_pairs={{0,16},{1,113},{2,18},{3,115},{4,20},{5,117},{6,22},{7,119},{8,24}... | collective-permute-start | bytes 2359304 | tf_op jit(solution)/shard_map/ppermute | solution.py:78
  69.6 30.3 %collective-permute-start.1 = (bf16[10,128,384]{2,1,0:T(8,128)(2,1)}, bf16[10,128,384]{2,1,0:T(8,128)(2,1)}, u32[]{:S(2)}, u32[]{:S(2)}) collective-permute-start(bf16[10,128,384]{2,1,0:T(8,128)(2,1)} %pack_last.1), channel_id=1, source_target_pairs={{0,128},{16,144},{32,160},{48,176},{64,192},{80,208},{96,224},{112... | collective-permute-start | bytes 2949128 | tf_op jit(solution)/shard_map/ppermute | solution.py:66
  72.0 16.3 %collective-permute-start.3 = (bf16[128,1536]{1,0:T(8,128)(2,1)}, bf16[128,1536]{1,0:T(8,128)(2,1)S(1)}, u32[]{:S(2)}, u32[]{:S(2)}) collective-permute-start(bf16[128,1536]{1,0:T(8,128)(2,1)} %get-tuple-element.39), channel_id=1, source_target_pairs={{0,32},{1,97},{2,34},{3,99},{4,36},{5,101},{6,38},{7,103},{8,40},{... | collective-permute-start | bytes 1179656 | tf_op jit(solution)/shard_map/ppermute | solution.py:78
  89.7 18.5 %collective-permute-start.5 = (bf16[2,128,1536]{2,1,0:T(8,128)(2,1)S(1)}, bf16[2,128,1536]{2,1,0:T(8,128)(2,1)S(1)}, u32[]{:S(2)}, u32[]{:S(2)}) collective-permute-start(bf16[2,128,1536]{2,1,0:T(8,128)(2,1)S(1)} %join_sums.1), channel_id=1, source_target_pairs={{0,16},{1,113},{2,18},{3,115},{4,20},{5,117},{6,22},{7,119},{8,24}... | collective-permute-start | bytes 2359304 | tf_op jit(solution)/shard_map/ppermute | solution.py:78
  93.5 24.1 %collective-permute-start.11 = (bf16[384,768]{1,0:T(8,128)(2,1)S(1)}, bf16[384,768]{1,0:T(8,128)(2,1)S(1)}, u32[]{:S(2)}, u32[]{:S(2)}) collective-permute-start(bf16[384,768]{1,0:T(8,128)(2,1)S(1)} %weight_sum.2), channel_id=1, source_target_pairs={{0,256},{256,0},{1,257},{257,1},{2,258},{258,2},{3,259},{259,3},{4... | collective-permute-start | bytes 1769480 | tf_op jit(solution)/shard_map/ppermute | solution.py:249
  103.0 28.2 %collective-permute-start.10 = (bf16[384,768]{1,0:T(8,128)(2,1)S(1)}, bf16[384,768]{1,0:T(8,128)(2,1)S(1)}, u32[]{:S(2)}, u32[]{:S(2)}) collective-permute-start(bf16[384,768]{1,0:T(8,128)(2,1)S(1)} %weight_sum.3), channel_id=1, source_target_pairs={{0,256},{256,0},{1,257},{257,1},{2,258},{258,2},{3,259},{259,3},{4... | collective-permute-start | bytes 1769480 | tf_op jit(solution)/shard_map/ppermute | solution.py:249
  108.5 22.7 %collective-permute-start.6 = (bf16[128,768]{1,0:T(8,128)(2,1)S(1)}, bf16[128,768]{1,0:T(8,128)(2,1)S(1)}, u32[]{:S(2)}, u32[]{:S(2)}) collective-permute-start(bf16[128,768]{1,0:T(8,128)(2,1)S(1)} %get-tuple-element.57), channel_id=1, source_target_pairs={{0,16},{1,113},{2,18},{3,115},{4,20},{5,117},{6,22},{7,119},{8,24}... | collective-permute-start | bytes 589832 | tf_op jit(solution)/shard_map/ppermute | solution.py:78
  111.0 20.3 %collective-permute-start.7 = (bf16[128,768]{1,0:T(8,128)(2,1)S(1)}, bf16[128,768]{1,0:T(8,128)(2,1)S(1)}, u32[]{:S(2)}, u32[]{:S(2)}) collective-permute-start(bf16[128,768]{1,0:T(8,128)(2,1)S(1)} %get-tuple-element.56), channel_id=1, source_target_pairs={{0,17},{1,112},{2,19},{3,114},{4,21},{5,116},{6,23},{7,118},{8,25}... | collective-permute-start | bytes 589832 | tf_op jit(solution)/shard_map/ppermute | solution.py:78
  112.9 18.3 %collective-permute-start.8 = (bf16[128,768]{1,0:T(8,128)(2,1)S(1)}, bf16[128,768]{1,0:T(8,128)(2,1)S(1)}, u32[]{:S(2)}, u32[]{:S(2)}) collective-permute-start(bf16[128,768]{1,0:T(8,128)(2,1)S(1)} %get-tuple-element.55), channel_id=1, source_target_pairs={{0,144},{1,241},{2,146},{3,243},{4,148},{5,245},{6,150},{7,247},{8... | collective-permute-start | bytes 589832 | tf_op jit(solution)/shard_map/ppermute | solution.py:78
  117.5 13.7 %collective-permute-start.9 = (bf16[128,768]{1,0:T(8,128)(2,1)S(1)}, bf16[128,768]{1,0:T(8,128)(2,1)S(1)}, u32[]{:S(2)}, u32[]{:S(2)}) collective-permute-start(bf16[128,768]{1,0:T(8,128)(2,1)S(1)} %get-tuple-element.54), channel_id=1, source_target_pairs={{0,145},{1,240},{2,147},{3,242},{4,149},{5,244},{6,151},{7,246},{8... | collective-permute-start | bytes 589832 | tf_op jit(solution)/shard_map/ppermute | solution.py:78
  131.4 1.1 copy-start.3
